TPU v7x, 256 devices: a whole 4x4x8 slice. The times are simulated.
256 devices in a mesh: section: 4 (over y), expert: 64 (over z, x, core).
Axes of the slice: x: 4, y: 4, z: 8, core: 2. Of those that a mesh axis runs over, the one named last changes fastest.
Arguments:
- tokens_fwd: bfloat16 [512, 7168], P('expert'), may hold values from -6 to 6
- tokens_rev: bfloat16 [512, 7168], P('expert'), may hold values from -6 to 6
- routes_fwd: int32 [4, 512, 2], P('section', 'expert'), may hold values from 0 to 7, all different within a row; in each aligned block of 8 rows (0 to 7, 8 to 15, ..., all dimensions but the last counted through in order) at most 2 rows name the same one
- routes_rev: int32 [4, 512, 2], P('section', 'expert'), may hold values from 0 to 7, all different within a row; in each aligned block of 8 rows (0 to 7, 8 to 15, ..., all dimensions but the last counted through in order) at most 2 rows name the same one
- weights_fwd: bfloat16 [4, 512, 2], P('section', 'expert'), may hold values from 0.19921875 to 1
- weights_rev: bfloat16 [4, 512, 2], P('section', 'expert'), may hold values from 0.19921875 to 1
- norm_gain: bfloat16 [4, 7168], P('section'), may hold values from 0.5 to 1.5
- gate_proj: bfloat16 [4, 7168, 16384], P('section', None, 'expert'), may hold values from -0.0625 to 0.0625
- up_proj: bfloat16 [4, 7168, 16384], P('section', None, 'expert'), may hold values from -0.0625 to 0.0625
- down_proj: bfloat16 [4, 16384, 7168], P('section', 'expert'), may hold values from -0.125 to 0.125
Outputs:
- stash_fwd: bfloat16 [4, 512, 7168], P('section', 'expert')
- stash_rev: bfloat16 [4, 512, 7168], P('section', 'expert')
Inputs may be any that keep to these rules, and one draw needn't show every extreme that they name: `routes_fwd`: each token names 2 different experts, and among the 8 tokens of one device of expert (aligned blocks of rows) at one section every expert is named by exactly 2 tokens. `routes_rev`: each token names 2 different experts, and among the 8 tokens of one device of expert (aligned blocks of rows) at one section every expert is named by exactly 2 tokens.
All inputs are finite; a program needn't handle non-finite values.
Results may differ from a plain program's by a relative error of at most 0.02.
Values may be sent and summed in bfloat16 or wider, within the bound.
A program may use at most 64 MiB of HBM per device.

v0:
```python
import jax
import jax.numpy as jnp
from jax import lax
from jax.sharding import PartitionSpec as P

LIVE = 8
TOPK = 2


def from_behind(value, axis, steps):
    count = lax.axis_size(axis)
    leading, last = (max(0, -steps), min(count, count - steps))
    return lax.ppermute(value, axis, [(source, source + steps) for source in range(leading, last)])


def pick_slots(column, slots):
    count = column.shape[-1]
    order_key = jnp.where(column > 0, 0, count) + jnp.arange(count, dtype=jnp.int32)
    return jnp.argsort(order_key, axis=-1)[..., :slots]


def moe_layer(tokens, routes, weights, gain_row, gate_w, up_w, down_w, group_size, axis_count):
    tok_count = tokens.shape[0]
    width = tokens.shape[1]
    slots = tok_count * TOPK // LIVE
    floats = tokens.astype(jnp.float32)
    scale = lax.rsqrt(jnp.mean(floats * floats, axis=-1, keepdims=True) + 1e-06)
    normed = (floats * scale * gain_row.astype(jnp.float32)).astype(jnp.bfloat16)
    experts = jnp.arange(LIVE, dtype=jnp.int32)
    table = jnp.sum(
        weights.astype(jnp.float32)[:, :, None]
        * (routes[:, :, None] == experts[None, None, :]).astype(jnp.float32),
        axis=1,
    )
    table_low = table.astype(jnp.bfloat16)
    own_slots = pick_slots(table.T, slots)
    picked_rows = normed[own_slots]
    picked_weight = jnp.take_along_axis(table_low.T, own_slots, axis=1)
    owner_expert = jnp.arange(axis_count, dtype=jnp.int32) // group_size
    outgoing = jnp.take(picked_rows, owner_expert, axis=0)
    outgoing_weight = jnp.take(picked_weight, owner_expert, axis=0)
    rows = lax.all_to_all(outgoing, "expert", split_axis=0, concat_axis=0, tiled=True)
    row_weight = lax.all_to_all(outgoing_weight, "expert", split_axis=0, concat_axis=0, tiled=True)
    senders = rows.shape[0]
    items = rows.shape[1]
    flat = rows.reshape(senders * items, width)
    gate = jnp.dot(flat, gate_w, preferred_element_type=jnp.float32)
    up_val = jnp.dot(flat, up_w, preferred_element_type=jnp.float32)
    act = (jax.nn.silu(gate) * up_val * row_weight.reshape(-1, 1).astype(jnp.float32)).astype(
        jnp.bfloat16
    )
    product = jnp.dot(act, down_w, preferred_element_type=jnp.float32).astype(jnp.bfloat16)
    exchanged = product.reshape(senders, items, width)
    returned = lax.all_to_all(exchanged, "expert", split_axis=0, concat_axis=0, tiled=True)
    summed = jnp.sum(returned.astype(jnp.float32).reshape(LIVE, group_size, slots, width), axis=1)
    branch = (
        jnp.zeros((tok_count, width), jnp.float32)
        .at[own_slots.reshape(-1)]
        .add(summed.reshape(-1, width))
    )
    return (floats + branch).astype(jnp.bfloat16)


def body(
    tokens_fwd,
    tokens_rev,
    routes_fwd,
    routes_rev,
    weights_fwd,
    weights_rev,
    norm_gain,
    gate_proj,
    up_proj,
    down_proj,
):
    section_count = lax.axis_size("section")
    section_here = lax.axis_index("section")
    axis_count = lax.axis_size("expert")
    group_size = axis_count // LIVE
    held_fwd = tokens_fwd
    held_rev = tokens_rev
    stash_one = jnp.zeros_like(tokens_fwd)
    stash_two = jnp.zeros_like(tokens_rev)
    for moment in range(section_count):
        take_fwd = section_here == moment
        take_rev = section_here == section_count - 1 - moment
        current = jnp.where(take_fwd, held_fwd, held_rev)
        routes_now = jnp.where(take_fwd, routes_fwd[0], routes_rev[0])
        weights_now = jnp.where(take_fwd, weights_fwd[0], weights_rev[0])
        result = moe_layer(
            current,
            routes_now,
            weights_now,
            norm_gain[0],
            gate_proj[0],
            up_proj[0],
            down_proj[0],
            group_size,
            axis_count,
        )
        stash_one = jnp.where(take_fwd, result, stash_one)
        stash_two = jnp.where(take_rev, result, stash_two)
        held_fwd = from_behind(result, "section", 1)
        held_rev = from_behind(result, "section", -1)
    return (stash_one[None], stash_two[None])


def solution(mesh):
    placed = (
        P("expert", None),
        P("expert", None),
        P("section", "expert", None),
        P("section", "expert", None),
        P("section", "expert", None),
        P("section", "expert", None),
        P("section", None),
        P("section", None, "expert"),
        P("section", None, "expert"),
        P("section", "expert", None),
    )
    return jax.shard_map(
        body,
        mesh=mesh,
        in_specs=placed,
        out_specs=(P("section", "expert", None), P("section", "expert", None)),
        check_vma=False,
    )
```

profile of v0, /device:TPU:33, one launch (start us, length us, event | category | flops | bytes accessed | tf_op | source)
XLA Modules:
  0.0 608.4 jit_solution(5178378112100827400)
XLA Ops:
  12.8 11.9 %all-to-all-start.1 = ((bf16[64,1,2]{2,1,0:T(2,128)(2,1)}), bf16[64,1,2]{2,1,0:T(2,128)(2,1)S(1)}, u32[]{:S(2)}, u32[]{:S(2)}) async-start(bf16[64,1,2]{2,1,0:T(2,128)(2,1)} %copy.96), calls=%async_computation.1 | async-start | bytes 65536 | tf_op jit(solution)/shard_map/all_to_all | solution.py:43
  25.9 4.2 gather_fusion.4
  33.1 10.9 %all-to-all-start = ((bf16[64,2,7168]{2,1,0:T(2,128)(2,1)}), bf16[64,2,7168]{2,1,0:T(2,128)(2,1)}, u32[]{:S(2)}, u32[]{:S(2)}) async-start(bf16[64,2,7168]{2,1,0:T(2,128)(2,1)} %broadcast_select_fusion.3), calls=%async_computation | async-start | bytes 3670016 | tf_op jit(solution)/shard_map/all_to_all | solution.py:42
  44.3 44.0 %all-to-all-done = bf16[64,2,7168]{2,1,0:T(2,128)(2,1)} async-done(((bf16[64,2,7168]{2,1,0:T(2,128)(2,1)}), bf16[64,2,7168]{2,1,0:T(2,128)(2,1)}, u32[]{:S(2)}, u32[]{:S(2)}) %all-to-all-start) | async-done | bytes 1835040 | tf_op jit(solution)/shard_map/all_to_all | solution.py:42
  95.1 6.6 %convolution_convert_fusion.3 = bf16[128,7168]{1,0:T(8,128)(2,1)} fusion(bf16[1,256,7168]{2,1,0:T(8,128)(2,1)} %param.25, bf16[128,7168]{1,0:T(8,128)(2,1)S(1)} %reshape.391, bf16[1,7168,256]{2,1,0:T(8,128)(2,1)} %param.24, f32[128,256]{1,0:T(8,128)S(1)} %fusion.18, f32[128]{0:T(128)S(1)} %reshape.419), kind=kOutput, calls=%fused_computation.23 | convolution fusion | flops 940670976 | bytes 11141632 | tf_op jit(solution)/shard_map/dot_general | solution.py:52
  101.6 4.7 reshape.392
  106.4 6.6 %all-to-all-start.2 = ((bf16[64,2,7168]{2,1,0:T(2,128)(2,1)}), bf16[64,2,7168]{2,1,0:T(2,128)(2,1)S(1)}, u32[]{:S(2)}, u32[]{:S(2)}) async-start(bf16[64,2,7168]{2,1,0:T(2,128)(2,1)} %reshape.392), calls=%async_computation.2 | async-start | bytes 3670016 | tf_op jit(solution)/shard_map/all_to_all | solution.py:54
  113.0 44.4 %all-to-all-done.2 = bf16[64,2,7168]{2,1,0:T(2,128)(2,1)S(1)} async-done(((bf16[64,2,7168]{2,1,0:T(2,128)(2,1)}), bf16[64,2,7168]{2,1,0:T(2,128)(2,1)S(1)}, u32[]{:S(2)}, u32[]{:S(2)}) %all-to-all-start.2) | async-done | bytes 1835040 | tf_op jit(solution)/shard_map/all_to_all | solution.py:54
  165.8 7.5 %all-to-all-start.4 = ((bf16[64,1,2]{2,1,0:T(2,128)(2,1)}), bf16[64,1,2]{2,1,0:T(2,128)(2,1)S(1)}, u32[]{:S(2)}, u32[]{:S(2)}) async-start(bf16[64,1,2]{2,1,0:T(2,128)(2,1)} %copy.101), calls=%async_computation.4 | async-start | bytes 65536 | tf_op jit(solution)/shard_map/all_to_all | solution.py:43
  181.7 10.5 %all-to-all-start.3 = ((bf16[64,2,7168]{2,1,0:T(2,128)(2,1)}), bf16[64,2,7168]{2,1,0:T(2,128)(2,1)}, u32[]{:S(2)}, u32[]{:S(2)}) async-start(bf16[64,2,7168]{2,1,0:T(2,128)(2,1)} %broadcast_select_fusion.2), calls=%async_computation.3 | async-start | bytes 3670016 | tf_op jit(solution)/shard_map/all_to_all | solution.py:42
  192.4 44.2 %all-to-all-done.3 = bf16[64,2,7168]{2,1,0:T(2,128)(2,1)} async-done(((bf16[64,2,7168]{2,1,0:T(2,128)(2,1)}), bf16[64,2,7168]{2,1,0:T(2,128)(2,1)}, u32[]{:S(2)}, u32[]{:S(2)}) %all-to-all-start.3) | async-done | bytes 1835040 | tf_op jit(solution)/shard_map/all_to_all | solution.py:42
  243.4 6.6 %convolution_convert_fusion.2 = bf16[128,7168]{1,0:T(8,128)(2,1)} fusion(bf16[1,256,7168]{2,1,0:T(8,128)(2,1)} %param.25, bf16[128,7168]{1,0:T(8,128)(2,1)S(1)} %reshape.397, bf16[1,7168,256]{2,1,0:T(8,128)(2,1)} %param.24, f32[128,256]{1,0:T(8,128)S(1)} %fusion.16, f32[128]{0:T(128)S(1)} %reshape.423), kind=kOutput, calls=%fused_computation.22 | convolution fusion | flops 940670976 | bytes 11141632 | tf_op jit(solution)/shard_map/dot_general | solution.py:52
  249.9 4.7 reshape.398
  254.7 6.7 %all-to-all-start.5 = ((bf16[64,2,7168]{2,1,0:T(2,128)(2,1)}), bf16[64,2,7168]{2,1,0:T(2,128)(2,1)S(1)}, u32[]{:S(2)}, u32[]{:S(2)}) async-start(bf16[64,2,7168]{2,1,0:T(2,128)(2,1)} %reshape.398), calls=%async_computation.5 | async-start | bytes 3670016 | tf_op jit(solution)/shard_map/all_to_all | solution.py:54
  261.5 44.4 %all-to-all-done.5 = bf16[64,2,7168]{2,1,0:T(2,128)(2,1)S(1)} async-done(((bf16[64,2,7168]{2,1,0:T(2,128)(2,1)}), bf16[64,2,7168]{2,1,0:T(2,128)(2,1)S(1)}, u32[]{:S(2)}, u32[]{:S(2)}) %all-to-all-start.5) | async-done | bytes 1835040 | tf_op jit(solution)/shard_map/all_to_all | solution.py:54
  309.2 4.3 collective-permute-start.2
  315.4 6.8 %all-to-all-start.7 = ((bf16[64,1,2]{2,1,0:T(2,128)(2,1)}), bf16[64,1,2]{2,1,0:T(2,128)(2,1)S(1)}, u32[]{:S(2)}, u32[]{:S(2)}) async-start(bf16[64,1,2]{2,1,0:T(2,128)(2,1)} %copy.106), calls=%async_computation.7 | async-start | bytes 65536 | tf_op jit(solution)/shard_map/all_to_all | solution.py:43
  330.6 10.9 %all-to-all-start.6 = ((bf16[64,2,7168]{2,1,0:T(2,128)(2,1)}), bf16[64,2,7168]{2,1,0:T(2,128)(2,1)}, u32[]{:S(2)}, u32[]{:S(2)}) async-start(bf16[64,2,7168]{2,1,0:T(2,128)(2,1)} %broadcast_select_fusion.1), calls=%async_computation.6 | async-start | bytes 3670016 | tf_op jit(solution)/shard_map/all_to_all | solution.py:42
  341.7 44.0 %all-to-all-done.6 = bf16[64,2,7168]{2,1,0:T(2,128)(2,1)} async-done(((bf16[64,2,7168]{2,1,0:T(2,128)(2,1)}), bf16[64,2,7168]{2,1,0:T(2,128)(2,1)}, u32[]{:S(2)}, u32[]{:S(2)}) %all-to-all-start.6) | async-done | bytes 1835040 | tf_op jit(solution)/shard_map/all_to_all | solution.py:42
  392.5 6.6 %convolution_convert_fusion.1 = bf16[128,7168]{1,0:T(8,128)(2,1)} fusion(bf16[1,256,7168]{2,1,0:T(8,128)(2,1)} %param.25, bf16[128,7168]{1,0:T(8,128)(2,1)S(1)} %reshape.403, bf16[1,7168,256]{2,1,0:T(8,128)(2,1)} %param.24, f32[128,256]{1,0:T(8,128)S(1)} %fusion.14, f32[128]{0:T(128)S(1)} %reshape.427), kind=kOutput, calls=%fused_computation.21 | convolution fusion | flops 940670976 | bytes 11141632 | tf_op jit(solution)/shard_map/dot_general | solution.py:52
  399.0 4.7 reshape.404
  403.8 6.6 %all-to-all-start.8 = ((bf16[64,2,7168]{2,1,0:T(2,128)(2,1)}), bf16[64,2,7168]{2,1,0:T(2,128)(2,1)S(1)}, u32[]{:S(2)}, u32[]{:S(2)}) async-start(bf16[64,2,7168]{2,1,0:T(2,128)(2,1)} %reshape.404), calls=%async_computation.8 | async-start | bytes 3670016 | tf_op jit(solution)/shard_map/all_to_all | solution.py:54
  410.5 44.4 %all-to-all-done.8 = bf16[64,2,7168]{2,1,0:T(2,128)(2,1)S(1)} async-done(((bf16[64,2,7168]{2,1,0:T(2,128)(2,1)}), bf16[64,2,7168]{2,1,0:T(2,128)(2,1)S(1)}, u32[]{:S(2)}, u32[]{:S(2)}) %all-to-all-start.8) | async-done | bytes 1835040 | tf_op jit(solution)/shard_map/all_to_all | solution.py:54
  458.1 4.3 collective-permute-start.4
  464.3 7.3 %all-to-all-start.10 = ((bf16[64,1,2]{2,1,0:T(2,128)(2,1)}), bf16[64,1,2]{2,1,0:T(2,128)(2,1)S(1)}, u32[]{:S(2)}, u32[]{:S(2)}) async-start(bf16[64,1,2]{2,1,0:T(2,128)(2,1)} %copy.111), calls=%async_computation.10 | async-start | bytes 65536 | tf_op jit(solution)/shard_map/all_to_all | solution.py:43
  472.9 4.2 gather_fusion.13
  480.1 10.5 %all-to-all-start.9 = ((bf16[64,2,7168]{2,1,0:T(2,128)(2,1)}), bf16[64,2,7168]{2,1,0:T(2,128)(2,1)}, u32[]{:S(2)}, u32[]{:S(2)}) async-start(bf16[64,2,7168]{2,1,0:T(2,128)(2,1)} %broadcast_select_fusion), calls=%async_computation.9 | async-start | bytes 3670016 | tf_op jit(solution)/shard_map/all_to_all | solution.py:42
  490.8 44.2 %all-to-all-done.9 = bf16[64,2,7168]{2,1,0:T(2,128)(2,1)} async-done(((bf16[64,2,7168]{2,1,0:T(2,128)(2,1)}), bf16[64,2,7168]{2,1,0:T(2,128)(2,1)}, u32[]{:S(2)}, u32[]{:S(2)}) %all-to-all-start.9) | async-done | bytes 1835040 | tf_op jit(solution)/shard_map/all_to_all | solution.py:42
  541.8 6.6 %convolution_convert_fusion = bf16[128,7168]{1,0:T(8,128)(2,1)} fusion(bf16[1,256,7168]{2,1,0:T(8,128)(2,1)} %param.25, bf16[128,7168]{1,0:T(8,128)(2,1)S(1)} %reshape.409, bf16[1,7168,256]{2,1,0:T(8,128)(2,1)} %param.24, f32[128,256]{1,0:T(8,128)S(1)} %fusion.12, f32[128]{0:T(128)S(1)} %reshape.431), kind=kOutput, calls=%fused_computation.20 | convolution fusion | flops 940670976 | bytes 11141632 | tf_op jit(solution)/shard_map/dot_general | solution.py:52
  548.3 4.7 reshape.410
  553.0 6.7 %all-to-all-start.11 = ((bf16[64,2,7168]{2,1,0:T(2,128)(2,1)}), bf16[64,2,7168]{2,1,0:T(2,128)(2,1)S(1)}, u32[]{:S(2)}, u32[]{:S(2)}) async-start(bf16[64,2,7168]{2,1,0:T(2,128)(2,1)} %reshape.410), calls=%async_computation.11 | async-start | bytes 3670016 | tf_op jit(solution)/shard_map/all_to_all | solution.py:54
  559.9 44.4 %all-to-all-done.11 = bf16[64,2,7168]{2,1,0:T(2,128)(2,1)S(1)} async-done(((bf16[64,2,7168]{2,1,0:T(2,128)(2,1)}), bf16[64,2,7168]{2,1,0:T(2,128)(2,1)S(1)}, u32[]{:S(2)}, u32[]{:S(2)}) %all-to-all-start.11) | async-done | bytes 1835040 | tf_op jit(solution)/shard_map/all_to_all | solution.py:54
  (167 shorter events, 87.6 us)
Async XLA Ops:
  8.8 15.9 %copy-start = (bf16[8,7168]{1,0:T(8,128)(2,1)S(1)}, bf16[8,7168]{1,0:T(8,128)(2,1)}, u32[]{:S(2)}) copy-start(bf16[8,7168]{1,0:T(8,128)(2,1)} %param.16) | copy-start | bytes 344068
  8.8 15.9 %copy-start.1 = (bf16[8,7168]{1,0:T(8,128)(2,1)S(1)}, bf16[8,7168]{1,0:T(8,128)(2,1)}, u32[]{:S(2)}) copy-start(bf16[8,7168]{1,0:T(8,128)(2,1)} %param.17) | copy-start | bytes 344068
  8.9 16.1 %copy-start.2 = (bf16[1,7168]{1,0:T(2,128)(2,1)S(1)}, bf16[1,7168]{1,0:T(2,128)(2,1)}, u32[]{:S(2)}) copy-start(bf16[1,7168]{1,0:T(2,128)(2,1)} %param.22) | copy-start | bytes 43012
  12.8 20.3 %all-to-all-start.1 = ((bf16[64,1,2]{2,1,0:T(2,128)(2,1)}), bf16[64,1,2]{2,1,0:T(2,128)(2,1)S(1)}, u32[]{:S(2)}, u32[]{:S(2)}) async-start(bf16[64,1,2]{2,1,0:T(2,128)(2,1)} %copy.96), calls=%async_computation.1 | async-start | bytes 65536 | tf_op jit(solution)/shard_map/all_to_all | solution.py:43
  33.1 55.2 %all-to-all-start = ((bf16[64,2,7168]{2,1,0:T(2,128)(2,1)}), bf16[64,2,7168]{2,1,0:T(2,128)(2,1)}, u32[]{:S(2)}, u32[]{:S(2)}) async-start(bf16[64,2,7168]{2,1,0:T(2,128)(2,1)} %broadcast_select_fusion.3), calls=%async_computation | async-start | bytes 3670016 | tf_op jit(solution)/shard_map/all_to_all | solution.py:42
  106.4 51.1 %all-to-all-start.2 = ((bf16[64,2,7168]{2,1,0:T(2,128)(2,1)}), bf16[64,2,7168]{2,1,0:T(2,128)(2,1)S(1)}, u32[]{:S(2)}, u32[]{:S(2)}) async-start(bf16[64,2,7168]{2,1,0:T(2,128)(2,1)} %reshape.392), calls=%async_computation.2 | async-start | bytes 3670016 | tf_op jit(solution)/shard_map/all_to_all | solution.py:54
  160.7 12.7 %collective-permute-start = (bf16[8,7168]{1,0:T(8,128)(2,1)S(1)}, bf16[8,7168]{1,0:T(8,128)(2,1)S(1)}, u32[]{:S(2)}, u32[]{:S(2)}) collective-permute-start(bf16[8,7168]{1,0:T(8,128)(2,1)S(1)} %convert_element_type.195), channel_id=1, source_target_pairs={{0,64},{64,128},{128,192},{1,65},{65,129},{129,193},{2,66},{66,130... | collective-permute-start | bytes 344072 | tf_op jit(solution)/shard_map/ppermute | solution.py:13
  163.9 9.5 %collective-permute-start.1 = (bf16[8,7168]{1,0:T(8,128)(2,1)S(1)}, bf16[8,7168]{1,0:T(8,128)(2,1)S(1)}, u32[]{:S(2)}, u32[]{:S(2)}) collective-permute-start(bf16[8,7168]{1,0:T(8,128)(2,1)S(1)} %convert_element_type.195), channel_id=1, source_target_pairs={{64,0},{128,64},{192,128},{65,1},{129,65},{193,129},{66,2},{130,66... | collective-permute-start | bytes 344072 | tf_op jit(solution)/shard_map/ppermute | solution.py:13
  165.8 15.9 %all-to-all-start.4 = ((bf16[64,1,2]{2,1,0:T(2,128)(2,1)}), bf16[64,1,2]{2,1,0:T(2,128)(2,1)S(1)}, u32[]{:S(2)}, u32[]{:S(2)}) async-start(bf16[64,1,2]{2,1,0:T(2,128)(2,1)} %copy.101), calls=%async_computation.4 | async-start | bytes 65536 | tf_op jit(solution)/shard_map/all_to_all | solution.py:43
  181.7 54.9 %all-to-all-start.3 = ((bf16[64,2,7168]{2,1,0:T(2,128)(2,1)}), bf16[64,2,7168]{2,1,0:T(2,128)(2,1)}, u32[]{:S(2)}, u32[]{:S(2)}) async-start(bf16[64,2,7168]{2,1,0:T(2,128)(2,1)} %broadcast_select_fusion.2), calls=%async_computation.3 | async-start | bytes 3670016 | tf_op jit(solution)/shard_map/all_to_all | solution.py:42
  254.7 51.3 %all-to-all-start.5 = ((bf16[64,2,7168]{2,1,0:T(2,128)(2,1)}), bf16[64,2,7168]{2,1,0:T(2,128)(2,1)S(1)}, u32[]{:S(2)}, u32[]{:S(2)}) async-start(bf16[64,2,7168]{2,1,0:T(2,128)(2,1)} %reshape.398), calls=%async_computation.5 | async-start | bytes 3670016 | tf_op jit(solution)/shard_map/all_to_all | solution.py:54
  309.2 13.1 %collective-permute-start.2 = (bf16[8,7168]{1,0:T(8,128)(2,1)S(1)}, bf16[8,7168]{1,0:T(8,128)(2,1)S(1)}, u32[]{:S(2)}, u32[]{:S(2)}) collective-permute-start(bf16[8,7168]{1,0:T(8,128)(2,1)S(1)} %convert_element_type.206), channel_id=1, source_target_pairs={{0,64},{64,128},{128,192},{1,65},{65,129},{129,193},{2,66},{66,130... | collective-permute-start | bytes 344072 | tf_op jit(solution)/shard_map/ppermute | solution.py:13
  313.4 8.9 %collective-permute-start.3 = (bf16[8,7168]{1,0:T(8,128)(2,1)S(1)}, bf16[8,7168]{1,0:T(8,128)(2,1)S(1)}, u32[]{:S(2)}, u32[]{:S(2)}) collective-permute-start(bf16[8,7168]{1,0:T(8,128)(2,1)S(1)} %convert_element_type.206), channel_id=1, source_target_pairs={{64,0},{128,64},{192,128},{65,1},{129,65},{193,129},{66,2},{130,66... | collective-permute-start | bytes 344072 | tf_op jit(solution)/shard_map/ppermute | solution.py:13
  315.4 15.2 %all-to-all-start.7 = ((bf16[64,1,2]{2,1,0:T(2,128)(2,1)}), bf16[64,1,2]{2,1,0:T(2,128)(2,1)S(1)}, u32[]{:S(2)}, u32[]{:S(2)}) async-start(bf16[64,1,2]{2,1,0:T(2,128)(2,1)} %copy.106), calls=%async_computation.7 | async-start | bytes 65536 | tf_op jit(solution)/shard_map/all_to_all | solution.py:43
  330.6 55.1 %all-to-all-start.6 = ((bf16[64,2,7168]{2,1,0:T(2,128)(2,1)}), bf16[64,2,7168]{2,1,0:T(2,128)(2,1)}, u32[]{:S(2)}, u32[]{:S(2)}) async-start(bf16[64,2,7168]{2,1,0:T(2,128)(2,1)} %broadcast_select_fusion.1), calls=%async_computation.6 | async-start | bytes 3670016 | tf_op jit(solution)/shard_map/all_to_all | solution.py:42
  403.8 51.1 %all-to-all-start.8 = ((bf16[64,2,7168]{2,1,0:T(2,128)(2,1)}), bf16[64,2,7168]{2,1,0:T(2,128)(2,1)S(1)}, u32[]{:S(2)}, u32[]{:S(2)}) async-start(bf16[64,2,7168]{2,1,0:T(2,128)(2,1)} %reshape.404), calls=%async_computation.8 | async-start | bytes 3670016 | tf_op jit(solution)/shard_map/all_to_all | solution.py:54
  458.1 13.7 %collective-permute-start.4 = (bf16[8,7168]{1,0:T(8,128)(2,1)S(1)}, bf16[8,7168]{1,0:T(8,128)(2,1)S(1)}, u32[]{:S(2)}, u32[]{:S(2)}) collective-permute-start(bf16[8,7168]{1,0:T(8,128)(2,1)S(1)} %convert_element_type.217), channel_id=1, source_target_pairs={{0,64},{64,128},{128,192},{1,65},{65,129},{129,193},{2,66},{66,130... | collective-permute-start | bytes 344072 | tf_op jit(solution)/shard_map/ppermute | solution.py:13
  462.4 9.4 %collective-permute-start.5 = (bf16[8,7168]{1,0:T(8,128)(2,1)S(1)}, bf16[8,7168]{1,0:T(8,128)(2,1)S(1)}, u32[]{:S(2)}, u32[]{:S(2)}) collective-permute-start(bf16[8,7168]{1,0:T(8,128)(2,1)S(1)} %convert_element_type.217), channel_id=1, source_target_pairs={{64,0},{128,64},{192,128},{65,1},{129,65},{193,129},{66,2},{130,66... | collective-permute-start | bytes 344072 | tf_op jit(solution)/shard_map/ppermute | solution.py:13
  464.3 15.7 %all-to-all-start.10 = ((bf16[64,1,2]{2,1,0:T(2,128)(2,1)}), bf16[64,1,2]{2,1,0:T(2,128)(2,1)S(1)}, u32[]{:S(2)}, u32[]{:S(2)}) async-start(bf16[64,1,2]{2,1,0:T(2,128)(2,1)} %copy.111), calls=%async_computation.10 | async-start | bytes 65536 | tf_op jit(solution)/shard_map/all_to_all | solution.py:43
  480.1 54.9 %all-to-all-start.9 = ((bf16[64,2,7168]{2,1,0:T(2,128)(2,1)}), bf16[64,2,7168]{2,1,0:T(2,128)(2,1)}, u32[]{:S(2)}, u32[]{:S(2)}) async-start(bf16[64,2,7168]{2,1,0:T(2,128)(2,1)} %broadcast_select_fusion), calls=%async_computation.9 | async-start | bytes 3670016 | tf_op jit(solution)/shard_map/all_to_all | solution.py:42
  553.0 51.3 %all-to-all-start.11 = ((bf16[64,2,7168]{2,1,0:T(2,128)(2,1)}), bf16[64,2,7168]{2,1,0:T(2,128)(2,1)S(1)}, u32[]{:S(2)}, u32[]{:S(2)}) async-start(bf16[64,2,7168]{2,1,0:T(2,128)(2,1)} %reshape.410), calls=%async_computation.11 | async-start | bytes 3670016 | tf_op jit(solution)/shard_map/all_to_all | solution.py:54
where the time goes:
time: 619 us; the launch traced here: 608 us
  waiting for transfers between devices  354 us (57%)
  starting transfers between devices  118 us (19%)
  local copies, waits for them, and re-layouts  67.2 us (11%)
  matrix products  36.9 us (6%)
  other arithmetic  30 us (5%)
    all_to_all x4, waiting for transfers between devices, moe_layer(): lax.all_to_all(exchanged, 'expert', split_axis=0, concat_axis=0, tiled=True)  178 us
    all_to_all x4, waiting for transfers between devices, moe_layer(): lax.all_to_all(outgoing, 'expert', split_axis=0, concat_axis=0, tiled=True)  177 us
    all_to_all x4, starting transfers between devices, moe_layer(): lax.all_to_all(outgoing, 'expert', split_axis=0, concat_axis=0, tiled=True)  42.7 us
    all_to_all x4, starting transfers between devices, moe_layer(): lax.all_to_all(outgoing_weight, 'expert', split_axis=0, concat_axis=0, ti...  33.5 us
    all_to_all x4, starting transfers between devices, moe_layer(): lax.all_to_all(exchanged, 'expert', split_axis=0, concat_axis=0, tiled=True)  26.5 us
    dot_general x4, matrix products, moe_layer(): jnp.dot(act, down_w, preferred_element_type=jnp.float32)  26.2 us
    reshape x4, local copies, waits for them, and re-layouts, moe_layer(): exchanged = product.reshape(senders, items, width)  19 us
    gather x4, local copies, waits for them, and re-layouts, moe_layer(): outgoing = jnp.take(picked_rows, owner_expert, axis=0)  17 us
  transfers between devices with their start and end apart: 18, of which 8 were waited for; matrix products, arithmetic and copies ran while one was open for 6% of the time, Pallas kernels for 0%

commit v1 on v0

v1 whole, which is shorter than its diff:
```python
import functools

import jax
import jax.numpy as jnp
from jax import lax
from jax.experimental import pallas as pl
from jax.experimental.pallas import tpu as pltpu
from jax.sharding import PartitionSpec as P

MESH = pl.DeviceIdType.MESH
NS, NZ, NX, NC = 4, 8, 4, 2
NP = NX * NC
TOK = 8
SLOT = 2
D = 7168
PIECE = 256
FS = D // NP
HALF = D // NC
ROWS = NZ * NP * SLOT
BLK = NP * SLOT
PT = NP * TOK
BF, F32 = jnp.bfloat16, jnp.float32


def far_first(i):
    return 4 + (1 - 2 * (i % 2)) * ((i + 1) // 2)


def nt_dot(a, b):
    return lax.dot_general(a, b, (((1,), (1,)), ((), ())), preferred_element_type=F32)


def kernel(
    tokf_ref, tokr_ref, rf_ref, rr_ref, wf_ref, wr_ref, gain_ref, gate_hbm, up_hbm, down_hbm,
    outf_ref, outr_ref,
    wg, wu, wd, tall, tokx, xin, sown, snext, wcomb, rin, acc, ssq, guout, guin, act,
    pout, pown, pin, ret, retin, dout, dinit, xres, xnew, st_out, st_in,
    t_ss, t_rs, tok_ss, tok_rs, s_ss, s_rs, wl_s, w_ss, w_rs,
    d_ss, d_rs, di_ss, ag_ss, ag_rs, gu_ss, gu_rs, p_ss, p_rs, r_ss, r_rs, x_ss, x_rs, st_ss, st_rs,
):
    s = lax.axis_index("section")
    i = lax.axis_index("expert")
    z, p = i // NP, i % NP
    x, c = p // NC, p % NC
    outer = (s == 0) | (s == NS - 1)
    low = s < NS // 2

    def at(sec, zz, pp):
        return (sec, zz * NP + pp)

    def plane(r):
        return at(s, z, (p + r) % NP)

    def xpeer(d):
        return at(s, z, ((x + d) % NX) * NC + c)

    def zpeer(k):
        return at(s, (z + k) % NZ, p)

    sib = at(s, z, x * NC + 1 - c)
    up_sec, down_sec = (s + 1) % NS, (s + NS - 1) % NS

    def remote(src, dst, ss, rs, dev):
        return pltpu.make_async_remote_copy(
            src_ref=src, dst_ref=dst, send_sem=ss, recv_sem=rs, device_id=dev, device_id_type=MESH
        )

    def loop(n, f):
        def step(n_, carry):
            f(n_)
            return carry

        lax.fori_loop(0, n, step, 0)

    bar = pltpu.get_barrier_semaphore()

    def greet(dev):
        pl.semaphore_signal(bar, inc=1, device_id=dev, device_id_type=MESH)

    loop(NP - 1, lambda r: greet(plane(r + 1)))
    loop(NZ - 1, lambda k: greet(zpeer(k + 1)))
    loop(NZ, lambda k: greet(at(up_sec, (z + k) % NZ, p)))
    loop(NZ, lambda k: greet(at(down_sec, (z + k) % NZ, p)))

    def local_weights():
        cps = [
            pltpu.make_async_copy(gate_hbm.at[0, pl.ds(c * HALF, HALF), :], wg.at[c], wl_s.at[0]),
            pltpu.make_async_copy(up_hbm.at[0, pl.ds(c * HALF, HALF), :], wu.at[c], wl_s.at[1]),
        ]
        for q in range(NX):
            cps.append(
                pltpu.make_async_copy(
                    down_hbm.at[0, :, pl.ds(pl.multiple_of(c * HALF + q * FS, 128), FS)],
                    wd.at[q, pl.ds(c * PIECE, PIECE), :],
                    wl_s.at[2 + q],
                )
            )
        return cps

    def sibling_weights():
        o = 1 - c
        cps = [
            remote(gate_hbm.at[0, pl.ds(o * HALF, HALF), :], wg.at[c], w_ss.at[0], w_rs.at[0], sib),
            remote(up_hbm.at[0, pl.ds(o * HALF, HALF), :], wu.at[c], w_ss.at[1], w_rs.at[1], sib),
        ]
        for q in range(NX):
            cps.append(
                remote(
                    down_hbm.at[0, :, pl.ds(pl.multiple_of(o * HALF + q * FS, 128), FS)],
                    wd.at[q, pl.ds(c * PIECE, PIECE), :],
                    w_ss.at[2 + q],
                    w_rs.at[2 + q],
                    sib,
                )
            )
        return cps

    for cp in local_weights():
        cp.start()

    lane = lax.broadcasted_iota(jnp.int32, (TOK, 128), 1)
    for b, (routes, weights) in enumerate(((rf_ref, wf_ref), (rr_ref, wr_ref))):
        r0, r1 = routes[0, :, 0:1], routes[0, :, 1:2]
        w0, w1 = weights[0, :, 0:1].astype(F32), weights[0, :, 1:2].astype(F32)
        mask = jnp.where((r0 == lane) | (r1 == lane), 1.0, 0.0)
        wt = jnp.where(r0 == lane - NZ, w0, 0.0) + jnp.where(r1 == lane - NZ, w1, 0.0)
        tall[p, b * TOK : (b + 1) * TOK, :] = mask + wt

    @pl.when(outer)
    def _():
        first = s == 0
        for q in range(NP):
            f = (q % NC) * NX + q // NC
            sl = slice(f * FS, (f + 1) * FS)
            tokx[q] = jnp.where(first, tokf_ref[:, sl].astype(F32), tokr_ref[:, sl].astype(F32))

    pl.semaphore_wait(bar, NP - 1 + NZ - 1 + 2 * NZ)

    def t_copy(r):
        return remote(tall.at[p], tall.at[p], t_ss.at[r], t_rs.at[r], plane(r + 1))

    def t_wait(r):
        q = (p + NP - r - 1) % NP
        remote(tall.at[q], tall.at[q], t_ss.at[r], t_rs.at[r], plane(r + 1)).wait_recv()

    def tok_copy(r):
        return remote(tokx.at[(p + r + 1) % NP], xin.at[p], tok_ss.at[r], tok_rs.at[r], plane(r + 1))

    def tok_wait(r):
        q = (p + NP - r - 1) % NP
        remote(tokx.at[q], xin.at[q], tok_ss.at[r], tok_rs.at[r], plane(r + 1)).wait_recv()

    loop(NP - 1, lambda r: t_copy(r).start())

    @pl.when(outer)
    def _():
        loop(NP - 1, lambda r: tok_copy(r).start())

    for cp in sibling_weights():
        cp.start()

    @pl.when(outer)
    def _():
        xin[p] = tokx[p]

    loop(NP - 1, t_wait)

    row = lax.broadcasted_iota(jnp.int32, (ROWS, 128), 0)
    col = lax.broadcasted_iota(jnp.int32, (ROWS, 128), 1)
    pick = jnp.where(col == (z + row // BLK) % NZ, 1.0, 0.0)
    pick_w = jnp.where(col - NZ == (z + row // BLK) % NZ, 1.0, 0.0)
    ti = lax.broadcasted_iota(jnp.int32, (PT, PT), 0)
    tj = lax.broadcasted_iota(jnp.int32, (PT, PT), 1)
    before = jnp.where((ti // TOK == tj // TOK) & (tj < ti), 1.0, 0.0)
    srow = lax.broadcasted_iota(jnp.int32, (ROWS, PT), 0)
    scol = lax.broadcasted_iota(jnp.int32, (ROWS, PT), 1)
    trow = lax.broadcasted_iota(jnp.int32, (PT, ROWS), 0)
    tcol = lax.broadcasted_iota(jnp.int32, (PT, ROWS), 1)
    for b in range(2):
        t = tall[:, b * TOK : (b + 1) * TOK, :].reshape(PT, 128)
        rank = jnp.dot(before, t, preferred_element_type=F32)
        here = nt_dot(pick, t) * jnp.where(srow // SLOT % NP == scol // TOK, 1.0, 0.0)
        right = jnp.where(nt_dot(pick, rank) == (srow % SLOT).astype(F32), 1.0, 0.0)
        sown[b, :, 0:PT] = (here * right).astype(BF)
        sown[b, :, PT:128] = jnp.zeros((ROWS, 128 - PT), BF)
        here = nt_dot(t, pick_w) * jnp.where(tcol // SLOT % NP == trow // TOK, 1.0, 0.0)
        right = jnp.where(nt_dot(rank, pick) == (tcol % SLOT).astype(F32), 1.0, 0.0)
        wcomb[b] = (here * right).astype(BF)

    def s_copy(b):
        sec = down_sec if b == 0 else up_sec
        return remote(sown.at[b], snext.at[b], s_ss.at[b], s_rs.at[b], at(sec, z, p))

    for b in range(2):
        s_copy(b).start()

    def di_copy(k):
        return remote(dinit.at[k], rin.at[0, 0, (NZ - k) % NZ], di_ss.at[k], d_rs.at[0, (NZ - k) % NZ], zpeer(k))

    @pl.when(outer)
    def _():
        loop(NP - 1, tok_wait)
        xb = xin[...].reshape(PT, FS).astype(BF)
        xres[0] = xb
        sel = jnp.where(s == 0, sown[0, :, 0:PT], sown[1, :, 0:PT])
        picked = jnp.dot(sel, xb, preferred_element_type=F32).astype(BF)
        dinit[...] = picked.reshape(NZ, BLK, FS)
        loop(NZ - 1, lambda n: di_copy(far_first(n)).start())
        rin[0, 0, 0] = picked[0:BLK]

    def job(j, carry):
        b = jnp.where(low, j, 1 - j)
        step = 1 - 2 * b
        initial = outer & (j == 0)
        to = s + step
        has_next = (to >= 0) & (to < NS)
        to = jnp.clip(to, 0, NS - 1)
        jn = jnp.where(to < NS // 2, b, 1 - b)
        came = jnp.where(initial, s, jnp.clip(s - step, 0, NS - 1))

        def d_wait(k):
            remote(rin.at[j, 0, k], rin.at[j, 0, k], di_ss.at[k], d_rs.at[j, k], zpeer(4)).wait_recv()

        def ag_copy(d, k):
            return remote(
                rin.at[j, 0, k], rin.at[j, d, k], ag_ss.at[j, d - 1, k], ag_rs.at[j, d - 1, k], xpeer(d)
            )

        def relay(n):
            k = (NZ - far_first(n)) % NZ

            @pl.when(jnp.logical_not(initial & (k == 0)))
            def _():
                d_wait(k)

            for d in (2, 1, 3):
                ag_copy(d, k).start()

        loop(NZ, relay)

        @pl.when(j == 0)
        def _():
            cps = local_weights()
            cps[0].wait()
            cps[1].wait()
            cps = sibling_weights()
            cps[0].wait_recv()
            cps[1].wait_recv()

        def slice_product(d, first):
            q = (x + NX - d) % NX
            rows = rin[j, d].reshape(ROWS, FS).astype(F32)
            g = gain_ref[:, pl.ds(pl.multiple_of(c * HALF + q * FS, 128), FS)].astype(F32)
            ss = jnp.sum(rows * rows, axis=1, keepdims=True)
            u = (rows * g).astype(BF)
            at_row = pl.ds(pl.multiple_of(q * FS, 128), FS)
            for n, w in enumerate((wg, wu)):
                for h in range(NC):
                    sl = slice((n * NC + h) * PIECE, (n * NC + h + 1) * PIECE)
                    part = jnp.dot(u, w[h, at_row, :], preferred_element_type=F32)
                    acc[:, sl] = part if first else acc[:, sl] + part
            ss = jnp.broadcast_to(ss, (ROWS, 128))
            ssq[...] = ss if first else ssq[...] + ss

        slice_product(0, True)
        for d in (1, 3, 2):
            loop(NZ, lambda k, d=d: ag_copy(d, k).wait_recv())
            slice_product(d, False)

        wide = 2 * NC * PIECE
        guout[j, :, 0:wide] = acc[...].astype(BF)
        ss = ssq[...]
        hi = ss.astype(BF)
        lo = (ss - hi.astype(F32)).astype(BF)
        lanes = lax.broadcasted_iota(jnp.int32, (ROWS, 128), 1)
        guout[j, :, wide:] = jnp.where(lanes == 0, hi, lo)
        gu = remote(guout.at[j], guin.at[j], gu_ss.at[j], gu_rs.at[j], sib)
        gu.start()
        gu.wait_recv()
        ss = ss[:, 0:1] + guin[j, :, wide : wide + 1].astype(F32) + guin[j, :, wide + 1 : wide + 2].astype(F32)
        scale = lax.rsqrt(ss * (1.0 / D) + 1e-06)
        hid = NC * PIECE
        gate = (acc[:, 0:hid] + guin[j, :, 0:hid].astype(F32)) * scale
        upv = (acc[:, hid:wide] + guin[j, :, hid:wide].astype(F32)) * scale
        act[...] = (gate / (1.0 + jnp.exp(-gate)) * upv).astype(BF)

        @pl.when(j == 0)
        def _():
            for cp in local_weights()[2:]:
                cp.wait()
            for cp in sibling_weights()[2:]:
                cp.wait_recv()

        def p_copy(d, k):
            return remote(
                pout.at[j, d - 1, k], pin.at[j, d - 1, k], p_ss.at[j, d - 1, k], p_rs.at[j, d - 1, k], xpeer(d)
            )

        for d in (2, 1, 3, 0):
            part = jnp.dot(act[...], wd[(x + d) % NX], preferred_element_type=F32)
            if d:
                pout[j, d - 1] = part.astype(BF).reshape(NZ, BLK, FS)
                loop(NZ, lambda n, d=d: p_copy(d, far_first(n)).start())
            else:
                pown[...] = part.reshape(NZ, BLK, FS)

        def r_copy(k):
            return remote(
                ret.at[j, k], retin.at[j, (NZ - k) % NZ], r_ss.at[j, k], r_rs.at[j, (NZ - k) % NZ], zpeer(k)
            )

        def give_back(n):
            k = far_first(n)
            for d in (1, 2, 3):
                p_copy(d, k).wait_recv()
            total = pown[k]
            for d in (1, 2, 3):
                total = total + pin[j, d - 1, k].astype(F32)
            total = total.astype(BF)

            @pl.when(k != 0)
            def _():
                ret[j, k] = total
                r_copy(k).start()

            @pl.when(k == 0)
            def _():
                retin[j, 0] = total

        loop(NZ, give_back)

        def x_copy():
            return remote(xnew.at[j], xres.at[jn], x_ss.at[j], x_rs.at[jn], at(to, z, p))

        def r_wait(n):
            k = n + 1
            remote(retin.at[j, k], retin.at[j, k], r_ss.at[j, k], r_rs.at[j, k], zpeer(k)).wait_recv()

        @pl.when(jnp.logical_not(initial))
        def _():
            remote(xres.at[j], xres.at[j], x_ss.at[j], x_rs.at[j], at(came, z, p)).wait_recv()

        @pl.when(j == 0)
        def _():
            for b_ in range(2):
                s_copy(b_).wait_recv()

        loop(NZ - 1, r_wait)
        branch = jnp.dot(wcomb[b], retin[j].reshape(ROWS, FS), preferred_element_type=F32)
        fresh = (xres[j].astype(F32) + branch).astype(BF)

        @pl.when(has_next)
        def _():
            picked = jnp.dot(snext[b, :, 0:PT], fresh, preferred_element_type=F32).astype(BF)
            dout[j] = picked.reshape(NZ, BLK, FS)

            def send(n):
                k = far_first(n)
                remote(
                    dout.at[j, k], rin.at[jn, 0, (NZ - k) % NZ], d_ss.at[j, k], d_rs.at[jn, (NZ - k) % NZ],
                    at(to, (z + k) % NZ, p),
                ).start()

            loop(NZ, send)
            xnew[j] = fresh
            x_copy().start()

        st_out[j] = fresh.astype(F32).reshape(NP, TOK, FS)
        st_in[j, p] = st_out[j, p]

        def st_copy(r):
            return remote(
                st_out.at[j, (p + r + 1) % NP], st_in.at[j, p], st_ss.at[j, r], st_rs.at[j, r], plane(r + 1)
            )

        loop(NP - 1, lambda r: st_copy(r).start())

        return carry

    lax.fori_loop(0, 2, job, 0)

    def st_wait(n):
        j, r = n // (NP - 1), n % (NP - 1)
        q = (p + NP - r - 1) % NP
        remote(st_out.at[j, q], st_in.at[j, q], st_ss.at[j, r], st_rs.at[j, r], plane(r + 1)).wait()

    loop(2 * (NP - 1), st_wait)
    jf = jnp.where(low, 0, 1)
    for q in range(NP):
        f = (q % NC) * NX + q // NC
        outf_ref[0, :, f * FS : (f + 1) * FS] = st_in[jf, q].astype(BF)
        outr_ref[0, :, f * FS : (f + 1) * FS] = st_in[1 - jf, q].astype(BF)

    loop(NP - 1, lambda r: t_copy(r).wait_send())
    for b in range(2):
        s_copy(b).wait_send()
    for cp in sibling_weights():
        cp.wait_send()

    @pl.when(outer)
    def _():
        loop(NP - 1, lambda r: tok_copy(r).wait_send())
        loop(NZ - 1, lambda k: di_copy(k + 1).wait_send())

    def drain(j):
        b = jnp.where(low, j, 1 - j)
        to = s + 1 - 2 * b

        @pl.when((to >= 0) & (to < NS))
        def _():
            loop(NZ, lambda k: remote(dout.at[j, k], dout.at[j, k], d_ss.at[j, k], d_rs.at[j, k], zpeer(4)).wait_send())
            remote(xnew.at[j], xnew.at[j], x_ss.at[j], x_rs.at[j], zpeer(4)).wait_send()

        def ag(k):
            for d in (1, 2, 3):
                remote(rin.at[j, 0, k], rin.at[j, d, k], ag_ss.at[j, d - 1, k], ag_rs.at[j, d - 1, k], xpeer(d)).wait_send()
                remote(
                    pout.at[j, d - 1, k], pin.at[j, d - 1, k], p_ss.at[j, d - 1, k], p_rs.at[j, d - 1, k], xpeer(d)
                ).wait_send()

        loop(NZ, ag)
        remote(guout.at[j], guin.at[j], gu_ss.at[j], gu_rs.at[j], sib).wait_send()
        loop(
            NZ - 1,
            lambda k: remote(
                ret.at[j, k + 1], ret.at[j, k + 1], r_ss.at[j, k + 1], r_rs.at[j, k + 1], zpeer(4)
            ).wait_send(),
        )

    loop(2, drain)


def run(tokens_fwd, tokens_rev, routes_fwd, routes_rev, weights_fwd, weights_rev, norm_gain, gate_proj, up_proj, down_proj):
    vmem = pl.BlockSpec(memory_space=pltpu.VMEM)
    hbm = pl.BlockSpec(memory_space=pl.ANY)
    dma = pltpu.SemaphoreType.DMA
    out = jax.ShapeDtypeStruct((1, TOK, D), BF)
    wide = 2 * NC * PIECE
    return pl.pallas_call(
        kernel,
        name="moe_pipeline",
        out_shape=(out, out),
        in_specs=[vmem] * 7 + [hbm] * 3,
        out_specs=(vmem, vmem),
        scratch_shapes=[
            pltpu.VMEM((NC, HALF, PIECE), BF),
            pltpu.VMEM((NC, HALF, PIECE), BF),
            pltpu.VMEM((NX, NC * PIECE, FS), BF),
            pltpu.VMEM((NP, 2 * TOK, 128), F32),
            pltpu.VMEM((NP, TOK, FS), F32),
            pltpu.VMEM((NP, TOK, FS), F32),
            pltpu.VMEM((2, ROWS, 128), BF),
            pltpu.VMEM((2, ROWS, 128), BF),
            pltpu.VMEM((2, PT, ROWS), BF),
            pltpu.VMEM((2, NX, NZ, BLK, FS), BF),
            pltpu.VMEM((ROWS, wide), F32),
            pltpu.VMEM((ROWS, 128), F32),
            pltpu.VMEM((2, ROWS, wide + 128), BF),
            pltpu.VMEM((2, ROWS, wide + 128), BF),
            pltpu.VMEM((ROWS, NC * PIECE), BF),
            pltpu.VMEM((2, NX - 1, NZ, BLK, FS), BF),
            pltpu.VMEM((NZ, BLK, FS), F32),
            pltpu.VMEM((2, NX - 1, NZ, BLK, FS), BF),
            pltpu.VMEM((2, NZ, BLK, FS), BF),
            pltpu.VMEM((2, NZ, BLK, FS), BF),
            pltpu.VMEM((2, NZ, BLK, FS), BF),
            pltpu.VMEM((NZ, BLK, FS), BF),
            pltpu.VMEM((2, PT, FS), BF),
            pltpu.VMEM((2, PT, FS), BF),
            pltpu.VMEM((2, NP, TOK, FS), F32),
            pltpu.VMEM((2, NP, TOK, FS), F32),
            dma((NP - 1,)), dma((NP - 1,)), dma((NP - 1,)), dma((NP - 1,)), dma((2,)), dma((2,)),
            dma((2 + NX,)), dma((2 + NX,)), dma((2 + NX,)),
            dma((2, NZ)), dma((2, NZ)), dma((NZ,)),
            dma((2, NX - 1, NZ)), dma((2, NX - 1, NZ)), dma((2,)), dma((2,)),
            dma((2, NX - 1, NZ)), dma((2, NX - 1, NZ)), dma((2, NZ)), dma((2, NZ)),
            dma((2,)), dma((2,)), dma((2, NP - 1)), dma((2, NP - 1)),
        ],
        compiler_params=pltpu.CompilerParams(
            collective_id=0, has_side_effects=True, vmem_limit_bytes=56 * 2**20
        ),
    )(tokens_fwd, tokens_rev, routes_fwd, routes_rev, weights_fwd, weights_rev, norm_gain, gate_proj, up_proj, down_proj)


def solution(mesh):
    placed = (
        P("expert", None),
        P("expert", None),
        P("section", "expert", None),
        P("section", "expert", None),
        P("section", "expert", None),
        P("section", "expert", None),
        P("section", None),
        P("section", None, "expert"),
        P("section", None, "expert"),
        P("section", "expert", None),
    )
    return jax.shard_map(
        run,
        mesh=mesh,
        in_specs=placed,
        out_specs=(P("section", "expert", None), P("section", "expert", None)),
        check_vma=False,
    )
```

time: 619 us -> 181 us (0.29); the launches traced: 608 us -> 179 us
  waiting for transfers between devices: 354 us -> 0 us
  Pallas kernels: 0 us -> 170 us
  starting transfers between devices: 118 us -> 0 us
  local copies, waits for them, and re-layouts: 67.2 us -> 8.41 us
  matrix products: 36.9 us -> 0 us
  other arithmetic: 30 us -> 0 us
    all_to_all x12 -> x0, waiting for transfers between devices: 354 us -> none  [the longest x4 178 us: moe_layer(): lax.all_to_all(exchanged, 'expert', split_axis=0, concat_axis=0, tiled=True)]
    pallas_call x0 -> x1, Pallas kernels: none -> 170 us  [run(): pl.pallas_call(kernel, name='moe_pipeline', out_shape=(out, out), in_spec...]
    all_to_all x12 -> x0, starting transfers between devices: 103 us -> none  [the longest x4 42.7 us: moe_layer(): lax.all_to_all(outgoing, 'expert', split_axis=0, concat_axis=0, tiled=True)]
    dot_general x8 -> x0, matrix products: 36.9 us -> none  [the longest x4 26.2 us: moe_layer(): jnp.dot(act, down_w, preferred_element_type=jnp.float32)]
    reshape x16 -> x0, local copies, waits for them, and re-layouts: 36.8 us -> none  [the longest x4 19 us: moe_layer(): exchanged = product.reshape(senders, items, width)]
    gather x36 -> x0, local copies, waits for them, and re-layouts: 26.7 us -> none  [the longest x4 17 us: moe_layer(): outgoing = jnp.take(picked_rows, owner_expert, axis=0)]
    ppermute x6 -> x0, starting transfers between devices: 15.6 us -> none  [from_behind(): lax.ppermute(value, axis, [(source, source + steps) for source in range(l...]
    select_n x14 -> x0, other arithmetic: 12.6 us -> none  [the longest x5 11.8 us: moe_layer(): outgoing = jnp.take(picked_rows, owner_expert, axis=0)]
  transfers between devices with their start and end apart: 18 -> 0, of which waited for: 8 -> 0; matrix products, arithmetic and copies ran while one was open for 6% -> 0% of each run, Pallas kernels for 0% -> 0%
where the time goes in v1:
time: 181 us; the launch traced here: 179 us
  Pallas kernels  170 us (94%)
  local copies, waits for them, and re-layouts  8.41 us (5%)
    pallas_call x1, Pallas kernels, run(): pl.pallas_call(kernel, name='moe_pipeline', out_shape=(out, out), in_spec...  170 us
    unnamed x6, local copies, waits for them, and re-layouts  8.41 us

profile of v1, /device:TPU:33, one launch (start us, length us, event | category | flops | bytes accessed | tf_op | source)
XLA Modules:
  0.0 178.8 jit_solution(17598894814165987264)
XLA Ops:
  0.6 1.3 copy.14.wf_ref
  1.9 1.3 copy.15.wr_ref
  3.2 1.3 copy.12.rf_ref
  4.6 1.3 copy.13.rr_ref
  5.9 169.7 %moe_pipeline.1 = (bf16[1,8,7168]{2,1,0:T(8,128)(2,1)}, bf16[1,8,7168]{2,1,0:T(8,128)(2,1)}) custom-call(bf16[8,7168]{1,0:T(8,128)(2,1)} %tokf_ref.1, bf16[8,7168]{1,0:T(8,128)(2,1)} %tokr_ref.1, s32[1,8,2]{2,1,0:T(8,128)} %copy.12.rf_ref, s32[1,8,2]{2,1,0:T(8,128)} %copy.13.rr_ref, bf16[1,8,2]{2,1,0:T(8,128)(2,1)} %copy.14.wf_ref, ...), custom_call_target="tpu_custom_call" | custom-call | tf_op jit(solution)/shard_map/moe_pipeline/pallas_call | solution.py:439
  175.7 1.6 copy.18
  177.2 1.6 copy.19

commit v2 on v1

--- a/solution.py
+++ b/solution.py
@@ -11,6 +11,8 @@
 NS, NZ, NX, NC = 4, 8, 4, 2
 NP = NX * NC
 TOK = 8
+LIVE = NZ
+TOPK = 2
 SLOT = 2
 D = 7168
 PIECE = 256
@@ -19,11 +21,17 @@
 ROWS = NZ * NP * SLOT
 BLK = NP * SLOT
 PT = NP * TOK
+NH = 2
+NB = NZ // NH
+HROWS = ROWS // NH
+OFFSETS = ((4, 2, 6, 0), (3, 5, 1, 7))
+FAR_FIRST = (4, 3, 5, 2, 6, 1, 7, 0)
+GRP = 2
 BF, F32 = jnp.bfloat16, jnp.float32
 
 
-def far_first(i):
-    return 4 + (1 - 2 * (i % 2)) * ((i + 1) // 2)
+def place(k):
+    return OFFSETS[k % NH].index(-k % NZ)
 
 
 def nt_dot(a, b):
@@ -118,13 +126,17 @@
     for cp in local_weights():
         cp.start()
 
-    lane = lax.broadcasted_iota(jnp.int32, (TOK, 128), 1)
+    ei = lax.broadcasted_iota(jnp.int32, (2 * LIVE, TOK), 0)
+    eye = jnp.where(
+        lax.broadcasted_iota(jnp.int32, (TOK, TOK), 0) == lax.broadcasted_iota(jnp.int32, (TOK, TOK), 1), 1.0, 0.0
+    )
     for b, (routes, weights) in enumerate(((rf_ref, wf_ref), (rr_ref, wr_ref))):
-        r0, r1 = routes[0, :, 0:1], routes[0, :, 1:2]
-        w0, w1 = weights[0, :, 0:1].astype(F32), weights[0, :, 1:2].astype(F32)
-        mask = jnp.where((r0 == lane) | (r1 == lane), 1.0, 0.0)
-        wt = jnp.where(r0 == lane - NZ, w0, 0.0) + jnp.where(r1 == lane - NZ, w1, 0.0)
-        tall[p, b * TOK : (b + 1) * TOK, :] = mask + wt
+        turned = jnp.zeros((2 * LIVE, TOK), F32)
+        for n in range(TOPK):
+            route, weight = routes[n : n + 1, :], weights[n : n + 1, :].astype(F32)
+            turned += jnp.where(route == ei, 1.0, 0.0) + jnp.where(route == ei - LIVE, weight, 0.0)
+        tall[p, b * TOK : (b + 1) * TOK, :] = jnp.zeros((TOK, 128), F32)
+        tall[p, b * TOK : (b + 1) * TOK, 0 : 2 * LIVE] = nt_dot(eye, turned)
 
     @pl.when(outer)
     def _():
@@ -194,8 +206,10 @@
     for b in range(2):
         s_copy(b).start()
 
+    mine = z % NH
+
     def di_copy(k):
-        return remote(dinit.at[k], rin.at[0, 0, (NZ - k) % NZ], di_ss.at[k], d_rs.at[0, (NZ - k) % NZ], zpeer(k))
+        return remote(dinit.at[k], rin.at[0, mine, 0, place(k)], di_ss.at[k], d_rs.at[0, mine, place(k)], zpeer(k))
 
     @pl.when(outer)
     def _():
@@ -205,8 +219,9 @@
         sel = jnp.where(s == 0, sown[0, :, 0:PT], sown[1, :, 0:PT])
         picked = jnp.dot(sel, xb, preferred_element_type=F32).astype(BF)
         dinit[...] = picked.reshape(NZ, BLK, FS)
-        loop(NZ - 1, lambda n: di_copy(far_first(n)).start())
-        rin[0, 0, 0] = picked[0:BLK]
+        for k in FAR_FIRST[:-1]:
+            di_copy(k).start()
+        rin[0, mine, 0, place(0)] = picked[0:BLK]
 
     def job(j, carry):
         b = jnp.where(low, j, 1 - j)
@@ -218,25 +233,32 @@
         jn = jnp.where(to < NS // 2, b, 1 - b)
         came = jnp.where(initial, s, jnp.clip(s - step, 0, NS - 1))
 
-        def d_wait(k):
-            remote(rin.at[j, 0, k], rin.at[j, 0, k], di_ss.at[k], d_rs.at[j, k], zpeer(4)).wait_recv()
-
-        def ag_copy(d, k):
+        def offset(h, m):
+            return jnp.where(mine == h, OFFSETS[0][m], OFFSETS[1][m])
+
+        def d_wait(h, m):
+            here = rin.at[j, h, 0, m]
+            remote(here, here, di_ss.at[m], d_rs.at[j, h, m], zpeer(4)).wait_recv()
+
+        def ag_copy(h, d, m):
             return remote(
-                rin.at[j, 0, k], rin.at[j, d, k], ag_ss.at[j, d - 1, k], ag_rs.at[j, d - 1, k], xpeer(d)
+                rin.at[j, h, 0, m], rin.at[j, h, d, m], ag_ss.at[j, h, d - 1, m], ag_rs.at[j, h, d - 1, m], xpeer(d)
             )
 
-        def relay(n):
-            k = (NZ - far_first(n)) % NZ
-
-            @pl.when(jnp.logical_not(initial & (k == 0)))
-            def _():
-                d_wait(k)
-
-            for d in (2, 1, 3):
-                ag_copy(d, k).start()
-
-        loop(NZ, relay)
+        def relay(h):
+            for m in range(NB):
+                if OFFSETS[0][m] == 0:
+
+                    @pl.when(jnp.logical_not(initial & (mine == h)))
+                    def _():
+                        d_wait(h, m)
+                else:
+                    d_wait(h, m)
+                for d in (2, 1, 3):
+                    ag_copy(h, d, m).start()
+
+        for h in range(NH):
+            relay(h)
 
         @pl.when(j == 0)
         def _():
@@ -247,133 +269,141 @@
             cps[0].wait_recv()
             cps[1].wait_recv()
 
-        def slice_product(d, first):
+        wide, hid = 2 * NC * PIECE, NC * PIECE
+
+        def slice_product(h, d):
             q = (x + NX - d) % NX
-            rows = rin[j, d].reshape(ROWS, FS).astype(F32)
+            rows = rin[j, h, d].reshape(HROWS, FS).astype(F32)
             g = gain_ref[:, pl.ds(pl.multiple_of(c * HALF + q * FS, 128), FS)].astype(F32)
             ss = jnp.sum(rows * rows, axis=1, keepdims=True)
             u = (rows * g).astype(BF)
             at_row = pl.ds(pl.multiple_of(q * FS, 128), FS)
             for n, w in enumerate((wg, wu)):
-                for h in range(NC):
-                    sl = slice((n * NC + h) * PIECE, (n * NC + h + 1) * PIECE)
-                    part = jnp.dot(u, w[h, at_row, :], preferred_element_type=F32)
-                    acc[:, sl] = part if first else acc[:, sl] + part
-            ss = jnp.broadcast_to(ss, (ROWS, 128))
-            ssq[...] = ss if first else ssq[...] + ss
-
-        slice_product(0, True)
-        for d in (1, 3, 2):
-            loop(NZ, lambda k, d=d: ag_copy(d, k).wait_recv())
-            slice_product(d, False)
-
-        wide = 2 * NC * PIECE
-        guout[j, :, 0:wide] = acc[...].astype(BF)
-        ss = ssq[...]
-        hi = ss.astype(BF)
-        lo = (ss - hi.astype(F32)).astype(BF)
-        lanes = lax.broadcasted_iota(jnp.int32, (ROWS, 128), 1)
-        guout[j, :, wide:] = jnp.where(lanes == 0, hi, lo)
-        gu = remote(guout.at[j], guin.at[j], gu_ss.at[j], gu_rs.at[j], sib)
-        gu.start()
-        gu.wait_recv()
-        ss = ss[:, 0:1] + guin[j, :, wide : wide + 1].astype(F32) + guin[j, :, wide + 1 : wide + 2].astype(F32)
-        scale = lax.rsqrt(ss * (1.0 / D) + 1e-06)
-        hid = NC * PIECE
-        gate = (acc[:, 0:hid] + guin[j, :, 0:hid].astype(F32)) * scale
-        upv = (acc[:, hid:wide] + guin[j, :, hid:wide].astype(F32)) * scale
-        act[...] = (gate / (1.0 + jnp.exp(-gate)) * upv).astype(BF)
-
-        @pl.when(j == 0)
-        def _():
-            for cp in local_weights()[2:]:
-                cp.wait()
-            for cp in sibling_weights()[2:]:
-                cp.wait_recv()
-
-        def p_copy(d, k):
+                for o in range(NC):
+                    sl = slice((n * NC + o) * PIECE, (n * NC + o + 1) * PIECE)
+                    part = jnp.dot(u, w[o, at_row, :], preferred_element_type=F32)
+                    acc[:, sl] = acc[:, sl] + part if d else part
+            ss = jnp.broadcast_to(ss, (HROWS, 128))
+            ssq[...] = ssq[...] + ss if d else ss
+
+        def p_copy(h, d, g):
+            ks = pl.ds(g * GRP, GRP)
             return remote(
-                pout.at[j, d - 1, k], pin.at[j, d - 1, k], p_ss.at[j, d - 1, k], p_rs.at[j, d - 1, k], xpeer(d)
+                pout.at[j, h, d - 1, ks], pin.at[j, h, d - 1, ks], p_ss.at[j, h, d - 1, g], p_rs.at[j, h, d - 1, g], xpeer(d)
             )
 
-        for d in (2, 1, 3, 0):
-            part = jnp.dot(act[...], wd[(x + d) % NX], preferred_element_type=F32)
-            if d:
-                pout[j, d - 1] = part.astype(BF).reshape(NZ, BLK, FS)
-                loop(NZ, lambda n, d=d: p_copy(d, far_first(n)).start())
-            else:
-                pown[...] = part.reshape(NZ, BLK, FS)
-
-        def r_copy(k):
-            return remote(
-                ret.at[j, k], retin.at[j, (NZ - k) % NZ], r_ss.at[j, k], r_rs.at[j, (NZ - k) % NZ], zpeer(k)
-            )
-
-        def give_back(n):
-            k = far_first(n)
-            for d in (1, 2, 3):
-                p_copy(d, k).wait_recv()
-            total = pown[k]
-            for d in (1, 2, 3):
-                total = total + pin[j, d - 1, k].astype(F32)
-            total = total.astype(BF)
-
-            @pl.when(k != 0)
-            def _():
-                ret[j, k] = total
-                r_copy(k).start()
-
-            @pl.when(k == 0)
-            def _():
-                retin[j, 0] = total
-
-        loop(NZ, give_back)
+        def expert(h):
+            slice_product(h, 0)
+            for d in (1, 3, 2):
+                for m in range(NB):
+                    ag_copy(h, d, m).wait_recv()
+                slice_product(h, d)
+
+            guout[j, h, :, 0:wide] = acc[...].astype(BF)
+            ss = ssq[...]
+            hi = ss.astype(BF)
+            lo = (ss - hi.astype(F32)).astype(BF)
+            lanes = lax.broadcasted_iota(jnp.int32, (HROWS, 128), 1)
+            guout[j, h, :, wide:] = jnp.where(lanes == 0, hi, lo)
+            gu = remote(guout.at[j, h], guin.at[j, h], gu_ss.at[j, h], gu_rs.at[j, h], sib)
+            gu.start()
+            gu.wait_recv()
+            ss = ss[:, 0:1] + guin[j, h, :, wide : wide + 1].astype(F32) + guin[j, h, :, wide + 1 : wide + 2].astype(F32)
+            scale = lax.rsqrt(ss * (1.0 / D) + 1e-06)
+            gate = (acc[:, 0:hid] + guin[j, h, :, 0:hid].astype(F32)) * scale
+            upv = (acc[:, hid:wide] + guin[j, h, :, hid:wide].astype(F32)) * scale
+            act[...] = (gate / (1.0 + jnp.exp(-gate)) * upv).astype(BF)
+
+            if h == 0:
+
+                @pl.when(j == 0)
+                def _():
+                    for cp in local_weights()[2:]:
+                        cp.wait()
+                    for cp in sibling_weights()[2:]:
+                        cp.wait_recv()
+
+            for d in (2, 1, 3):
+                part = jnp.dot(act[...], wd[(x + d) % NX], preferred_element_type=F32)
+                pout[j, h, d - 1] = part.astype(BF).reshape(NB, BLK, FS)
+                for g in range(NB // GRP):
+                    p_copy(h, d, g).start()
+            pown[h] = jnp.dot(act[...], wd[x], preferred_element_type=F32).reshape(NB, BLK, FS)
+
+        for h in range(NH):
+            expert(h)
+
+        def r_copy(h, m, k):
+            kk = (NZ - k) % NZ
+            return remote(ret.at[j, h, m], retin.at[j, kk], r_ss.at[j, h, m], r_rs.at[j, kk], zpeer(k))
+
+        def give_back(h):
+            for g in range(NB // GRP):
+                for d in (1, 3, 2):
+                    p_copy(h, d, g).wait_recv()
+                for m in range(g * GRP, (g + 1) * GRP):
+                    total = pown[h, m]
+                    for d in (1, 2, 3):
+                        total = total + pin[j, h, d - 1, m].astype(F32)
+                    total = total.astype(BF)
+                    k = offset(h, m)
+                    if OFFSETS[0][m]:
+                        ret[j, h, m] = total
+                        r_copy(h, m, k).start()
+                    else:
+
+                        @pl.when(mine == h)
+                        def _():
+                            retin[j, 0] = total
+
+                        @pl.when(mine != h)
+                        def _():
+                            ret[j, h, m] = total
+                            r_copy(h, m, k).start()
 
         def x_copy():
             return remote(xnew.at[j], xres.at[jn], x_ss.at[j], x_rs.at[jn], at(to, z, p))
-
-        def r_wait(n):
-            k = n + 1
-            remote(retin.at[j, k], retin.at[j, k], r_ss.at[j, k], r_rs.at[j, k], zpeer(k)).wait_recv()
-
-        @pl.when(jnp.logical_not(initial))
-        def _():
-            remote(xres.at[j], xres.at[j], x_ss.at[j], x_rs.at[j], at(came, z, p)).wait_recv()
-
-        @pl.when(j == 0)
-        def _():
-            for b_ in range(2):
-                s_copy(b_).wait_recv()
-
-        loop(NZ - 1, r_wait)
-        branch = jnp.dot(wcomb[b], retin[j].reshape(ROWS, FS), preferred_element_type=F32)
-        fresh = (xres[j].astype(F32) + branch).astype(BF)
-
-        @pl.when(has_next)
-        def _():
-            picked = jnp.dot(snext[b, :, 0:PT], fresh, preferred_element_type=F32).astype(BF)
-            dout[j] = picked.reshape(NZ, BLK, FS)
-
-            def send(n):
-                k = far_first(n)
-                remote(
-                    dout.at[j, k], rin.at[jn, 0, (NZ - k) % NZ], d_ss.at[j, k], d_rs.at[jn, (NZ - k) % NZ],
-                    at(to, (z + k) % NZ, p),
-                ).start()
-
-            loop(NZ, send)
-            xnew[j] = fresh
-            x_copy().start()
-
-        st_out[j] = fresh.astype(F32).reshape(NP, TOK, FS)
-        st_in[j, p] = st_out[j, p]
 
         def st_copy(r):
             return remote(
                 st_out.at[j, (p + r + 1) % NP], st_in.at[j, p], st_ss.at[j, r], st_rs.at[j, r], plane(r + 1)
             )
 
-        loop(NP - 1, lambda r: st_copy(r).start())
+        def owner():
+            @pl.when(jnp.logical_not(initial))
+            def _():
+                remote(xres.at[j], xres.at[j], x_ss.at[j], x_rs.at[j], at(came, z, p)).wait_recv()
+
+            @pl.when(j == 0)
+            def _():
+                for b_ in range(2):
+                    s_copy(b_).wait_recv()
+
+            for k in range(1, NZ):
+                remote(retin.at[j, k], retin.at[j, k], r_ss.at[j, 0, 0], r_rs.at[j, k], zpeer(4)).wait_recv()
+            back = retin[j].reshape(ROWS, FS)
+            branch = jnp.dot(wcomb[b], back, preferred_element_type=F32)
+            fresh = (xres[j].astype(F32) + branch).astype(BF)
+
+            @pl.when(has_next)
+            def _():
+                picked = jnp.dot(snext[b, :, 0:PT], fresh, preferred_element_type=F32).astype(BF)
+                dout[j] = picked.reshape(NZ, BLK, FS)
+                for k in FAR_FIRST:
+                    remote(
+                        dout.at[j, k], rin.at[jn, mine, 0, place(k)], d_ss.at[j, k], d_rs.at[jn, mine, place(k)],
+                        at(to, (z + k) % NZ, p),
+                    ).start()
+                xnew[j] = fresh
+                x_copy().start()
+
+            st_out[j] = fresh.astype(F32).reshape(NP, TOK, FS)
+            st_in[j, p] = st_out[j, p]
+            loop(NP - 1, lambda r: st_copy(r).start())
+
+        for h in range(NH):
+            give_back(h)
+        owner()
 
         return carry
 
@@ -400,7 +430,8 @@
     @pl.when(outer)
     def _():
         loop(NP - 1, lambda r: tok_copy(r).wait_send())
-        loop(NZ - 1, lambda k: di_copy(k + 1).wait_send())
+        for k in range(1, NZ):
+            di_copy(k).wait_send()
 
     def drain(j):
         b = jnp.where(low, j, 1 - j)
@@ -408,24 +439,29 @@
 
         @pl.when((to >= 0) & (to < NS))
         def _():
-            loop(NZ, lambda k: remote(dout.at[j, k], dout.at[j, k], d_ss.at[j, k], d_rs.at[j, k], zpeer(4)).wait_send())
+            for k in range(NZ):
+                remote(dout.at[j, k], dout.at[j, k], d_ss.at[j, k], d_rs.at[j, 0, 0], zpeer(4)).wait_send()
             remote(xnew.at[j], xnew.at[j], x_ss.at[j], x_rs.at[j], zpeer(4)).wait_send()
 
-        def ag(k):
+        for h in range(NH):
+            for m in range(NB):
+                for d in (1, 2, 3):
+                    here = rin.at[j, h, 0, m]
+                    remote(here, here, ag_ss.at[j, h, d - 1, m], ag_rs.at[j, h, d - 1, m], xpeer(d)).wait_send()
+
+                def back_sent():
+                    here = ret.at[j, h, m]
+                    remote(here, here, r_ss.at[j, h, m], r_rs.at[j, m], zpeer(4)).wait_send()
+
+                if OFFSETS[0][m]:
+                    back_sent()
+                else:
+                    pl.when(mine != h)(back_sent)
             for d in (1, 2, 3):
-                remote(rin.at[j, 0, k], rin.at[j, d, k], ag_ss.at[j, d - 1, k], ag_rs.at[j, d - 1, k], xpeer(d)).wait_send()
-                remote(
-                    pout.at[j, d - 1, k], pin.at[j, d - 1, k], p_ss.at[j, d - 1, k], p_rs.at[j, d - 1, k], xpeer(d)
-                ).wait_send()
-
-        loop(NZ, ag)
-        remote(guout.at[j], guin.at[j], gu_ss.at[j], gu_rs.at[j], sib).wait_send()
-        loop(
-            NZ - 1,
-            lambda k: remote(
-                ret.at[j, k + 1], ret.at[j, k + 1], r_ss.at[j, k + 1], r_rs.at[j, k + 1], zpeer(4)
-            ).wait_send(),
-        )
+                for g in range(NB // GRP):
+                    here = pout.at[j, h, d - 1, pl.ds(g * GRP, GRP)]
+                    remote(here, here, p_ss.at[j, h, d - 1, g], p_rs.at[j, h, d - 1, g], xpeer(d)).wait_send()
+            remote(guout.at[j, h], guin.at[j, h], gu_ss.at[j, h], gu_rs.at[j, h], sib).wait_send()
 
     loop(2, drain)
 
@@ -436,6 +472,7 @@
     dma = pltpu.SemaphoreType.DMA
     out = jax.ShapeDtypeStruct((1, TOK, D), BF)
     wide = 2 * NC * PIECE
+    small = [a[0].T for a in (routes_fwd, routes_rev, weights_fwd, weights_rev)]
     return pl.pallas_call(
         kernel,
         name="moe_pipeline",
@@ -452,16 +489,16 @@
             pltpu.VMEM((2, ROWS, 128), BF),
             pltpu.VMEM((2, ROWS, 128), BF),
             pltpu.VMEM((2, PT, ROWS), BF),
-            pltpu.VMEM((2, NX, NZ, BLK, FS), BF),
-            pltpu.VMEM((ROWS, wide), F32),
-            pltpu.VMEM((ROWS, 128), F32),
-            pltpu.VMEM((2, ROWS, wide + 128), BF),
-            pltpu.VMEM((2, ROWS, wide + 128), BF),
-            pltpu.VMEM((ROWS, NC * PIECE), BF),
-            pltpu.VMEM((2, NX - 1, NZ, BLK, FS), BF),
-            pltpu.VMEM((NZ, BLK, FS), F32),
-            pltpu.VMEM((2, NX - 1, NZ, BLK, FS), BF),
-            pltpu.VMEM((2, NZ, BLK, FS), BF),
+            pltpu.VMEM((2, NH, NX, NB, BLK, FS), BF),
+            pltpu.VMEM((HROWS, wide), F32),
+            pltpu.VMEM((HROWS, 128), F32),
+            pltpu.VMEM((2, NH, HROWS, wide + 128), BF),
+            pltpu.VMEM((2, NH, HROWS, wide + 128), BF),
+            pltpu.VMEM((HROWS, NC * PIECE), BF),
+            pltpu.VMEM((2, NH, NX - 1, NB, BLK, FS), BF),
+            pltpu.VMEM((NH, NB, BLK, FS), F32),
+            pltpu.VMEM((2, NH, NX - 1, NB, BLK, FS), BF),
+            pltpu.VMEM((2, NH, NB, BLK, FS), BF),
             pltpu.VMEM((2, NZ, BLK, FS), BF),
             pltpu.VMEM((2, NZ, BLK, FS), BF),
             pltpu.VMEM((NZ, BLK, FS), BF),
@@ -471,15 +508,15 @@
             pltpu.VMEM((2, NP, TOK, FS), F32),
             dma((NP - 1,)), dma((NP - 1,)), dma((NP - 1,)), dma((NP - 1,)), dma((2,)), dma((2,)),
             dma((2 + NX,)), dma((2 + NX,)), dma((2 + NX,)),
-            dma((2, NZ)), dma((2, NZ)), dma((NZ,)),
-            dma((2, NX - 1, NZ)), dma((2, NX - 1, NZ)), dma((2,)), dma((2,)),
-            dma((2, NX - 1, NZ)), dma((2, NX - 1, NZ)), dma((2, NZ)), dma((2, NZ)),
+            dma((2, NZ)), dma((2, NH, NB)), dma((NZ,)),
+            dma((2, NH, NX - 1, NB)), dma((2, NH, NX - 1, NB)), dma((2, NH)), dma((2, NH)),
+            dma((2, NH, NX - 1, NB // GRP)), dma((2, NH, NX - 1, NB // GRP)), dma((2, NH, NB)), dma((2, NZ)),
             dma((2,)), dma((2,)), dma((2, NP - 1)), dma((2, NP - 1)),
         ],
         compiler_params=pltpu.CompilerParams(
             collective_id=0, has_side_effects=True, vmem_limit_bytes=56 * 2**20
         ),
-    )(tokens_fwd, tokens_rev, routes_fwd, routes_rev, weights_fwd, weights_rev, norm_gain, gate_proj, up_proj, down_proj)
+    )(tokens_fwd, tokens_rev, *small, norm_gain, gate_proj, up_proj, down_proj)
 
 
 def solution(mesh):

time: 181 us -> 151 us (0.83); the launches traced: 179 us -> 151 us
  Pallas kernels: 170 us -> 148 us
  local copies, waits for them, and re-layouts: 8.41 us -> 3.1 us
    pallas_call x1, Pallas kernels: 170 us -> 148 us  [run(): pl.pallas_call(kernel, name='moe_pipeline', out_shape=(out, out), in_spec...]
    unnamed x6 -> x2, local copies, waits for them, and re-layouts: 8.41 us -> 3.1 us
where the time goes in v2:
time: 151 us
  Pallas kernels  148 us (98%)
  local copies, waits for them, and re-layouts  3.1 us (2%)
    pallas_call x1, Pallas kernels, run(): pl.pallas_call(kernel, name='moe_pipeline', out_shape=(out, out), in_spec...  148 us
    unnamed x2, local copies, waits for them, and re-layouts  3.1 us

profile of v2, /device:TPU:33, one launch (start us, length us, event | category | flops | bytes accessed | tf_op | source)
XLA Modules:
  0.0 151.3 jit_solution(17818394027512137336)
XLA Ops:
  0.6 147.5 %moe_pipeline.1 = (bf16[1,8,7168]{2,1,0:T(8,128)(2,1)}, bf16[1,8,7168]{2,1,0:T(8,128)(2,1)}) custom-call(bf16[8,7168]{1,0:T(8,128)(2,1)} %tokf_ref.1, bf16[8,7168]{1,0:T(8,128)(2,1)} %tokr_ref.1, s32[2,8]{1,0:T(2,128)} %bitcast.12, s32[2,8]{1,0:T(2,128)} %bitcast.13, bf16[2,8]{1,0:T(2,128)(2,1)} %bitcast.14, bf16[2,8]{1,0:T(2,128)(2,1)} %bitcast.15, ...), custom_call_target="tpu_custom_call" | custom-call | tf_op jit(solution)/shard_map/moe_pipeline/pallas_call | solution.py:476
  148.2 1.6 %copy.14 = bf16[1,8,7168]{2,1,0:T(8,128)(2,1)} copy(bf16[1,8,7168]{2,1,0:T(8,128)(2,1)} %get-tuple-element.4) | data formatting | bytes 229376
  149.7 1.6 %copy.15 = bf16[1,8,7168]{2,1,0:T(8,128)(2,1)} copy(bf16[1,8,7168]{2,1,0:T(8,128)(2,1)} %get-tuple-element.5) | data formatting | bytes 229376

commit v3 on v2

v3 whole, which is shorter than its diff:
```python
import functools

import jax
import jax.numpy as jnp
from jax import lax
from jax.experimental import pallas as pl
from jax.experimental.pallas import tpu as pltpu
from jax.sharding import PartitionSpec as P

MESH = pl.DeviceIdType.MESH
NS, NZ, NX, NC = 4, 8, 4, 2
NP = NX * NC
TOK = 8
LIVE = NZ
TOPK = 2
SLOT = 2
D = 7168
PIECE = 256
FS = D // NP
HALF = D // NC
ROWS = NZ * NP * SLOT
BLK = NP * SLOT
PT = NP * TOK
NH = 2
NB = NZ // NH
HROWS = ROWS // NH
OFFSETS = ((4, 2, 6, 0), (3, 5, 1, 7))
FAR_FIRST = (4, 3, 5, 2, 6, 1, 7, 0)
GRP = 1
BF, F32 = jnp.bfloat16, jnp.float32


def place(k):
    return OFFSETS[k % NH].index(-k % NZ)


def nt_dot(a, b):
    return lax.dot_general(a, b, (((1,), (1,)), ((), ())), preferred_element_type=F32)


def kernel(
    tokf_hbm, tokr_hbm, rf_hbm, rr_hbm, wf_hbm, wr_hbm, gain_hbm, gate_hbm, up_hbm, down_hbm,
    out_ref,
    tok_ref, rf_ref, rr_ref, wf_ref, wr_ref, gain_ref, out_f32, in_s,
    wg, wu, wd, wall, tall, tokx, xin, sown, wcomb, wbefore, rin, acc, ssq, guout, guin, act, actin,
    pout, pown, pin, ret, retin, dout, xcur, xres, xback, st_out, st_in,
    t_ss, t_rs, tok_ss, tok_rs, s_ss, s_rs, wl_s, w_ss, w_rs, wa_l, wa_ss, wa_rs, a_ss, a_rs,
    d_ss, d_rs, ag_ss, ag_rs, gu_ss, gu_rs, p_ss, p_rs, r_ss, r_rs, x_ss, x_rs, xb_ss, xb_rs, st_ss, st_rs,
):
    s = lax.axis_index("section")
    i = lax.axis_index("expert")
    z, p = i // NP, i % NP
    x, c = p // NC, p % NC
    outer = (s == 0) | (s == NS - 1)
    low = s < NS // 2

    def at(sec, zz, pp):
        return (sec, zz * NP + pp)

    def plane(r):
        return at(s, z, (p + r) % NP)

    def xpeer(d):
        return at(s, z, ((x + d) % NX) * NC + c)

    def zpeer(k):
        return at(s, (z + k) % NZ, p)

    sib = at(s, z, x * NC + 1 - c)
    up_sec, down_sec = (s + 1) % NS, (s + NS - 1) % NS

    def remote(src, dst, ss, rs, dev):
        return pltpu.make_async_remote_copy(
            src_ref=src, dst_ref=dst, send_sem=ss, recv_sem=rs, device_id=dev, device_id_type=MESH
        )

    def loop(n, f):
        def step(n_, carry):
            f(n_)
            return carry

        lax.fori_loop(0, n, step, 0)

    small = [
        pltpu.make_async_copy(src, dst, in_s.at[n])
        for n, (src, dst) in enumerate(
            ((rf_hbm, rf_ref), (rr_hbm, rr_ref), (wf_hbm, wf_ref), (wr_hbm, wr_ref), (gain_hbm, gain_ref))
        )
    ]
    for cp in small:
        cp.start()
    tokens = [pltpu.make_async_copy(src, tok_ref, in_s.at[5]) for src in (tokf_hbm, tokr_hbm)]
    pl.when(s == 0)(lambda: tokens[0].start())
    pl.when(s == NS - 1)(lambda: tokens[1].start())
    bar = pltpu.get_barrier_semaphore()

    def greet(dev):
        pl.semaphore_signal(bar, inc=1, device_id=dev, device_id_type=MESH)

    loop(NP - 1, lambda r: greet(plane(r + 1)))
    loop(NZ - 1, lambda k: greet(zpeer(k + 1)))
    loop(NZ, lambda k: greet(at(up_sec, (z + k) % NZ, p)))
    loop(NZ, lambda k: greet(at(down_sec, (z + k) % NZ, p)))

    def half(core):
        return pl.ds(core * HALF, HALF)

    def slice_of(xx, core):
        return pl.ds(pl.multiple_of(core * HALF + xx * FS, 128), FS)

    def local_gate_up():
        return [
            pltpu.make_async_copy(gate_hbm.at[0, half(c), :], wg.at[c], wl_s.at[0]),
            pltpu.make_async_copy(up_hbm.at[0, half(c), :], wu.at[c], wl_s.at[1]),
        ]

    def sibling_gate_up():
        return [
            remote(gate_hbm.at[0, half(1 - c), :], wg.at[c], w_ss.at[0], w_rs.at[0], sib),
            remote(up_hbm.at[0, half(1 - c), :], wu.at[c], w_ss.at[1], w_rs.at[1], sib),
        ]

    def local_down(q):
        return pltpu.make_async_copy(
            down_hbm.at[0, :, slice_of(q, c)], wd.at[q, pl.ds(c * PIECE, PIECE), :], wl_s.at[2 + q]
        )

    def sibling_down(q):
        return remote(
            down_hbm.at[0, :, slice_of(q, 1 - c)], wd.at[q, pl.ds(c * PIECE, PIECE), :], w_ss.at[2 + q], w_rs.at[2 + q], sib
        )

    def local_spread():
        return pltpu.make_async_copy(down_hbm.at[0, :, slice_of(x, c)], wall.at[p], wa_l.at[0])

    def spread(r):
        q = (p + r + 1) % NP
        return remote(down_hbm.at[0, :, slice_of(q // NC, q % NC)], wall.at[p], wa_ss.at[0], wa_rs.at[0], plane(r + 1))

    def all_spread():
        some = wall.at[pl.ds(0, NP - 1)]
        return remote(some, some, wa_ss.at[0], wa_rs.at[0], sib)

    def start_spread():
        local_spread().start()
        loop(NP - 1, lambda r: spread(r).start())

    def wait_spread():
        local_spread().wait()
        all_spread().wait_recv()

    for cp in local_gate_up():
        cp.start()

    @pl.when(outer)
    def _():
        for q in range(NX):
            local_down(q).start()

    for cp in small:
        cp.wait()
    ei = lax.broadcasted_iota(jnp.int32, (2 * LIVE, TOK), 0)
    eye = jnp.where(
        lax.broadcasted_iota(jnp.int32, (TOK, TOK), 0) == lax.broadcasted_iota(jnp.int32, (TOK, TOK), 1), 1.0, 0.0
    )
    for b, (routes, weights) in enumerate(((rf_ref, wf_ref), (rr_ref, wr_ref))):
        turned = jnp.zeros((2 * LIVE, TOK), F32)
        for n in range(TOPK):
            route, weight = routes[n : n + 1, :], weights[n : n + 1, :].astype(F32)
            turned += jnp.where(route == ei, 1.0, 0.0) + jnp.where(route == ei - LIVE, weight, 0.0)
        tall[p, b * TOK : (b + 1) * TOK, :] = jnp.zeros((TOK, 128), F32)
        tall[p, b * TOK : (b + 1) * TOK, 0 : 2 * LIVE] = nt_dot(eye, turned)

    @pl.when(outer)
    def _():
        tokens[0].wait()
        for q in range(NP):
            f = (q % NC) * NX + q // NC
            sl = slice(f * FS, (f + 1) * FS)
            tokx[q] = tok_ref[:, sl].astype(F32)

    pl.semaphore_wait(bar, NP - 1 + NZ - 1 + 2 * NZ)

    def t_copy(r):
        return remote(tall.at[p], tall.at[p], t_ss.at[0], t_rs.at[0], plane(r + 1))

    few = pl.ds(0, NP - 1)

    def tok_copy(r):
        return remote(tokx.at[(p + r + 1) % NP], xin.at[p], tok_ss.at[0], tok_rs.at[0], plane(r + 1))

    loop(NP - 1, lambda r: t_copy(r).start())

    @pl.when(outer)
    def _():
        loop(NP - 1, lambda r: tok_copy(r).start())

    for cp in sibling_gate_up():
        cp.start()

    @pl.when(outer)
    def _():
        for q in range(NX):
            sibling_down(q).start()

    pl.when(jnp.logical_not(outer))(start_spread)

    @pl.when(outer)
    def _():
        xin[p] = tokx[p]

    remote(tall.at[few], tall.at[few], t_ss.at[0], t_rs.at[0], sib).wait_recv()

    row = lax.broadcasted_iota(jnp.int32, (ROWS, 128), 0)
    col = lax.broadcasted_iota(jnp.int32, (ROWS, 128), 1)
    pick = jnp.where(col == (z + row // BLK) % NZ, 1.0, 0.0)
    pick_w = jnp.where(col - NZ == (z + row // BLK) % NZ, 1.0, 0.0)
    ti = lax.broadcasted_iota(jnp.int32, (PT, PT), 0)
    tj = lax.broadcasted_iota(jnp.int32, (PT, PT), 1)
    before = jnp.where((ti // TOK == tj // TOK) & (tj < ti), 1.0, 0.0)
    srow = lax.broadcasted_iota(jnp.int32, (ROWS, PT), 0)
    scol = lax.broadcasted_iota(jnp.int32, (ROWS, PT), 1)
    trow = lax.broadcasted_iota(jnp.int32, (PT, ROWS), 0)
    tcol = lax.broadcasted_iota(jnp.int32, (PT, ROWS), 1)
    for b in range(2):
        t = tall[:, b * TOK : (b + 1) * TOK, :].reshape(PT, 128)
        rank = jnp.dot(before, t, preferred_element_type=F32)
        here = nt_dot(pick, t) * jnp.where(srow // SLOT % NP == scol // TOK, 1.0, 0.0)
        right = jnp.where(nt_dot(pick, rank) == (srow % SLOT).astype(F32), 1.0, 0.0)
        sown[b, :, 0:PT] = (here * right).astype(BF)
        sown[b, :, PT:128] = jnp.zeros((ROWS, 128 - PT), BF)
        here = nt_dot(t, pick_w) * jnp.where(tcol // SLOT % NP == trow // TOK, 1.0, 0.0)
        right = jnp.where(nt_dot(rank, pick) == (tcol % SLOT).astype(F32), 1.0, 0.0)
        wcomb[b] = (here * right).astype(BF)

    def w_copy(b):
        sec = up_sec if b == 0 else down_sec
        return remote(wcomb.at[b], wbefore.at[b], s_ss.at[b], s_rs.at[b], at(sec, z, p))

    for b in range(2):
        w_copy(b).start()

    @pl.when(outer)
    def _():
        remote(tokx.at[few], xin.at[few], tok_ss.at[0], tok_rs.at[0], sib).wait_recv()
        xcur[0] = xin[...].reshape(PT, FS).astype(BF)

    mine = z % NH

    def st_copy(j, r):
        return remote(
            st_out.at[j, (p + r + 1) % NP], st_in.at[j, p], st_ss.at[j], st_rs.at[j], plane(r + 1)
        )

    def stash(j, value):
        st_out[j] = value.astype(F32).reshape(NP, TOK, FS)
        st_in[j, p] = st_out[j, p]
        loop(NP - 1, lambda r: st_copy(j, r).start())

    def finish(j):
        remote(st_out.at[j, few], st_in.at[j, few], st_ss.at[j], st_rs.at[j], sib).wait_recv()
        for q in range(NP):
            f = (q % NC) * NX + q // NC
            out_f32[j, :, f * FS : (f + 1) * FS] = st_in[j, q]

    def stash_back(j):
        remote(xback.at[j], xback.at[j], xb_ss.at[j], xb_rs.at[j], zpeer(4)).wait_recv()
        stash(j, xback[j])

    def w_wait():
        for b in range(2):
            w_copy(b).wait_recv()

    def job(j, carry):
        b = jnp.where(low, j, 1 - j)
        step = 1 - 2 * b
        initial = outer & (j == 0)
        to = s + step
        has_next = (to >= 0) & (to < NS)
        to = jnp.clip(to, 0, NS - 1)
        jn = jnp.where(to < NS // 2, b, 1 - b)
        came = jnp.clip(s - step, 0, NS - 1)
        jc = jnp.where(came < NS // 2, b, 1 - b)
        dest, slot = jnp.where(has_next, to, s), jnp.where(has_next, jn, 2)

        @pl.when(jnp.logical_not(initial))
        def _():
            pl.when(j == 0)(w_wait)
            remote(xres.at[j], xres.at[j], x_ss.at[j], x_rs.at[j], zpeer(4)).wait_recv()
            remote(retin.at[j], retin.at[j], r_ss.at[j, 0], r_rs.at[j], zpeer(4)).wait_recv()
            branch = jnp.dot(wbefore[b], retin[j].reshape(ROWS, FS), preferred_element_type=F32)
            xcur[j] = (xres[j].astype(F32) + branch).astype(BF)

        picked = jnp.dot(sown[b, :, 0:PT], xcur[j], preferred_element_type=F32).astype(BF)
        dout[j] = picked.reshape(NZ, BLK, FS)
        for k in FAR_FIRST[:-1]:
            remote(
                dout.at[j, k], rin.at[j, mine, 0, place(k)], d_ss.at[j], d_rs.at[j, mine, place(k)], zpeer(k)
            ).start()
        rin[j, mine, 0, place(0)] = picked[0:BLK]

        @pl.when(has_next)
        def _():
            remote(xcur.at[j], xres.at[jn], x_ss.at[j], x_rs.at[jn], at(to, z, p)).start()

        @pl.when(jnp.logical_not(initial))
        def _():
            remote(xcur.at[j], xback.at[jc], xb_ss.at[j], xb_rs.at[jc], at(came, z, p)).start()

        def offset(h, m):
            return jnp.where(mine == h, OFFSETS[0][m], OFFSETS[1][m])

        def d_wait(h, m):
            here = rin.at[j, h, 0, m]
            remote(here, here, d_ss.at[j], d_rs.at[j, h, m], zpeer(4)).wait_recv()

        def ag_copy(h, d, m):
            return remote(
                rin.at[j, h, 0, m], rin.at[j, h, d, m], ag_ss.at[j, h, d - 1], ag_rs.at[j, h, d - 1], xpeer(d)
            )

        def relay(h):
            for m in range(NB):
                if OFFSETS[0][m] == 0:

                    @pl.when(mine != h)
                    def _():
                        d_wait(h, m)
                else:
                    d_wait(h, m)
                for d in (2, 1, 3):
                    ag_copy(h, d, m).start()

        for h in range(NH):
            relay(h)

        @pl.when(j == 0)
        def _():
            for cp in local_gate_up():
                cp.wait()
            for cp in sibling_gate_up():
                cp.wait_recv()

        wide, hid = 2 * NC * PIECE, NC * PIECE

        def slice_product(h, d):
            q = (x + NX - d) % NX
            rows = rin[j, h, d].reshape(HROWS, FS).astype(F32)
            g = gain_ref[:, pl.ds(pl.multiple_of(c * HALF + q * FS, 128), FS)].astype(F32)
            ss = jnp.sum(rows * rows, axis=1, keepdims=True)
            u = (rows * g).astype(BF)
            at_row = pl.ds(pl.multiple_of(q * FS, 128), FS)
            for n, w in enumerate((wg, wu)):
                for o in range(NC):
                    sl = slice((n * NC + o) * PIECE, (n * NC + o + 1) * PIECE)
                    part = jnp.dot(u, w[o, at_row, :], preferred_element_type=F32)
                    acc[:, sl] = acc[:, sl] + part if d else part
            ss = jnp.broadcast_to(ss, (HROWS, 128))
            ssq[...] = ssq[...] + ss if d else ss

        def p_copy(h, d, g):
            ks = pl.ds(g * GRP, GRP)
            return remote(
                pout.at[h, d - 1, ks], pin.at[h, d - 1, ks], p_ss.at[h, d - 1], p_rs.at[h, d - 1, g], xpeer(d)
            )

        def act_copy(h, d):
            return remote(act.at[j, h], actin.at[j, h, d - 1], a_ss.at[j, h, d - 1], a_rs.at[j, h, d - 1], xpeer(d))

        def all_of(value, q):
            w = wall[pl.ds(q * NC, NC)].reshape(NC * PIECE, FS)
            return jnp.dot(value, w, preferred_element_type=F32).reshape(NB, BLK, FS)

        def expert(h):
            slice_product(h, 0)
            for d in (1, 3, 2):
                remote(rin.at[j, h, 0], rin.at[j, h, d], ag_ss.at[j, h, d - 1], ag_rs.at[j, h, d - 1], sib).wait_recv()
                slice_product(h, d)

            guout[j, h, :, 0:wide] = acc[...].astype(BF)
            ss = ssq[...]
            hi = ss.astype(BF)
            lo = (ss - hi.astype(F32)).astype(BF)
            lanes = lax.broadcasted_iota(jnp.int32, (HROWS, 128), 1)
            guout[j, h, :, wide:] = jnp.where(lanes == 0, hi, lo)
            gu = remote(guout.at[j, h], guin.at[j, h], gu_ss.at[j, h], gu_rs.at[j, h], sib)
            gu.start()
            gu.wait_recv()
            ss = ss[:, 0:1] + guin[j, h, :, wide : wide + 1].astype(F32) + guin[j, h, :, wide + 1 : wide + 2].astype(F32)
            scale = lax.rsqrt(ss * (1.0 / D) + 1e-06)
            gate = (acc[:, 0:hid] + guin[j, h, :, 0:hid].astype(F32)) * scale
            upv = (acc[:, hid:wide] + guin[j, h, :, hid:wide].astype(F32)) * scale
            act[j, h] = (gate / (1.0 + jnp.exp(-gate)) * upv).astype(BF)

            @pl.when(initial)
            def _():
                if h == 0:
                    for q in range(NX):
                        local_down(q).wait()
                        sibling_down(q).wait_recv()
                for d in (2, 1, 3):
                    part = jnp.dot(act[j, h], wd[(x + d) % NX], preferred_element_type=F32)
                    pout[h, d - 1] = part.astype(BF).reshape(NB, BLK, FS)
                for g in range(NB // GRP):
                    for d in (2, 1, 3):
                        p_copy(h, d, g).start()
                pown[h] = jnp.dot(act[j, h], wd[x], preferred_element_type=F32).reshape(NB, BLK, FS)

            @pl.when(jnp.logical_not(initial))
            def _():
                for d in (2, 1, 3):
                    act_copy(h, d).start()
                if h == 0:
                    pl.when((j == 0) | outer)(wait_spread)
                pown[h] = all_of(act[j, h], x)

        for h in range(NH):
            expert(h)

        pl.when(j == 1)(lambda: stash_back(0))

        def r_copy(h, m, k):
            kk = (NZ - k) % NZ
            return remote(
                ret.at[j, h, m], retin.at[slot, kk], r_ss.at[j, h], r_rs.at[slot], at(dest, (z + k) % NZ, p)
            )

        def hand(h, m, total):
            k = offset(h, m)
            total = total.astype(BF)
            if OFFSETS[0][m]:
                ret[j, h, m] = total
                r_copy(h, m, k).start()
            else:
                here = (mine == h) & jnp.logical_not(has_next)

                @pl.when(here)
                def _():
                    retin[2, 0] = total

                @pl.when(jnp.logical_not(here))
                def _():
                    ret[j, h, m] = total
                    r_copy(h, m, k).start()

        def give_back(h):
            @pl.when(initial)
            def _():
                for g in range(NB // GRP):
                    for d in (1, 3, 2):
                        p_copy(h, d, g).wait_recv()
                    for m in range(g * GRP, (g + 1) * GRP):
                        total = pown[h, m]
                        for d in (1, 2, 3):
                            total = total + pin[h, d - 1, m].astype(F32)
                        hand(h, m, total)

            @pl.when(jnp.logical_not(initial))
            def _():
                total = pown[h]
                for d in (1, 3, 2):
                    act_copy(h, d).wait_recv()
                    total = total + all_of(actin[j, h, d - 1], (x + NX - d) % NX)
                for m in range(NB):
                    hand(h, m, total[m])

        for h in range(NH):
            give_back(h)
        pl.when(initial)(w_wait)
        pl.when(initial)(start_spread)
        pl.when(j == 1)(lambda: finish(0))

        @pl.when(jnp.logical_not(has_next))
        def _():
            others = retin.at[2, pl.ds(1, NZ - 1)]
            remote(others, others, r_ss.at[j, 0], r_rs.at[2], zpeer(4)).wait_recv()
            branch = jnp.dot(wcomb[b], retin[2].reshape(ROWS, FS), preferred_element_type=F32)
            stash(j, (xcur[j].astype(F32) + branch).astype(BF))

        return carry

    lax.fori_loop(0, 2, job, 0)
    pl.when(jnp.logical_not(outer))(lambda: stash_back(1))

    finish(1)
    jf = jnp.where(low, 0, 1)
    out_ref[0:TOK, :] = out_f32[jf].astype(BF)
    out_ref[TOK : 2 * TOK, :] = out_f32[1 - jf].astype(BF)

    for j in range(2):
        remote(st_out.at[j, few], st_in.at[j, few], st_ss.at[j], st_rs.at[j], sib).wait_send()
    remote(tall.at[few], tall.at[few], t_ss.at[0], t_rs.at[0], sib).wait_send()
    for b in range(2):
        w_copy(b).wait_send()
    for cp in sibling_gate_up():
        cp.wait_send()
    all_spread().wait_send()

    @pl.when(outer)
    def _():
        remote(tokx.at[few], xin.at[few], tok_ss.at[0], tok_rs.at[0], sib).wait_send()
        for q in range(NX):
            sibling_down(q).wait_send()
        for h in range(NH):
            for d in (1, 2, 3):
                here = pout.at[h, d - 1]
                remote(here, here, p_ss.at[h, d - 1], p_rs.at[h, d - 1, 0], xpeer(d)).wait_send()

    def drain(j):
        b = jnp.where(low, j, 1 - j)
        to = s + 1 - 2 * b
        has_next = (to >= 0) & (to < NS)

        sent = dout.at[j, pl.ds(1, NZ - 1)]
        remote(sent, sent, d_ss.at[j], d_rs.at[j, 0, 0], zpeer(4)).wait_send()

        @pl.when(has_next)
        def _():
            remote(xcur.at[j], xcur.at[j], x_ss.at[j], x_rs.at[j], zpeer(4)).wait_send()

        @pl.when(jnp.logical_not(outer & (j == 0)))
        def _():
            remote(xcur.at[j], xcur.at[j], xb_ss.at[j], xb_rs.at[j], zpeer(4)).wait_send()

        for h in range(NH):
            for d in (1, 2, 3):
                here = rin.at[j, h, 0]
                remote(here, here, ag_ss.at[j, h, d - 1], ag_rs.at[j, h, d - 1], xpeer(d)).wait_send()

            here, fewer = ret.at[j, h], ret.at[j, h, pl.ds(0, NB - 1)]
            whole = (mine != h) | has_next
            pl.when(whole)(lambda: remote(here, here, r_ss.at[j, h], r_rs.at[j], zpeer(4)).wait_send())
            pl.when(jnp.logical_not(whole))(lambda: remote(fewer, fewer, r_ss.at[j, h], r_rs.at[j], zpeer(4)).wait_send())

            @pl.when(jnp.logical_not(outer & (j == 0)))
            def _():
                for d in (1, 2, 3):
                    here = act.at[j, h]
                    remote(here, here, a_ss.at[j, h, d - 1], a_rs.at[j, h, d - 1], xpeer(d)).wait_send()

            remote(guout.at[j, h], guin.at[j, h], gu_ss.at[j, h], gu_rs.at[j, h], sib).wait_send()

    loop(2, drain)


def split(both_ref, outf_ref, outr_ref):
    outf_ref[0] = both_ref[0:TOK, :]
    outr_ref[0] = both_ref[TOK : 2 * TOK, :]


def run(tokens_fwd, tokens_rev, routes_fwd, routes_rev, weights_fwd, weights_rev, norm_gain, gate_proj, up_proj, down_proj):
    vmem = pl.BlockSpec(memory_space=pltpu.VMEM)
    hbm = pl.BlockSpec(memory_space=pl.ANY)
    dma = pltpu.SemaphoreType.DMA
    out = jax.ShapeDtypeStruct((2 * TOK, D), BF)
    wide = 2 * NC * PIECE
    small = [a[0].T for a in (routes_fwd, routes_rev, weights_fwd, weights_rev)]
    both = pl.pallas_call(
        kernel,
        name="moe_pipeline",
        out_shape=out,
        in_specs=[hbm] * 10,
        out_specs=vmem,
        scratch_shapes=[
            pltpu.VMEM((TOK, D), BF),
            pltpu.VMEM((TOPK, TOK), jnp.int32),
            pltpu.VMEM((TOPK, TOK), jnp.int32),
            pltpu.VMEM((TOPK, TOK), BF),
            pltpu.VMEM((TOPK, TOK), BF),
            pltpu.VMEM((1, D), BF),
            pltpu.VMEM((2, TOK, D), F32),
            dma((6,)),
            pltpu.VMEM((NC, HALF, PIECE), BF),
            pltpu.VMEM((NC, HALF, PIECE), BF),
            pltpu.VMEM((NX, NC * PIECE, FS), BF),
            pltpu.VMEM((NP, PIECE, FS), BF),
            pltpu.VMEM((NP, 2 * TOK, 128), F32),
            pltpu.VMEM((NP, TOK, FS), F32),
            pltpu.VMEM((NP, TOK, FS), F32),
            pltpu.VMEM((2, ROWS, 128), BF),
            pltpu.VMEM((2, PT, ROWS), BF),
            pltpu.VMEM((2, PT, ROWS), BF),
            pltpu.VMEM((2, NH, NX, NB, BLK, FS), BF),
            pltpu.VMEM((HROWS, wide), F32),
            pltpu.VMEM((HROWS, 128), F32),
            pltpu.VMEM((2, NH, HROWS, wide + 128), BF),
            pltpu.VMEM((2, NH, HROWS, wide + 128), BF),
            pltpu.VMEM((2, NH, HROWS, NC * PIECE), BF),
            pltpu.VMEM((2, NH, NX - 1, HROWS, NC * PIECE), BF),
            pltpu.VMEM((NH, NX - 1, NB, BLK, FS), BF),
            pltpu.VMEM((NH, NB, BLK, FS), F32),
            pltpu.VMEM((NH, NX - 1, NB, BLK, FS), BF),
            pltpu.VMEM((2, NH, NB, BLK, FS), BF),
            pltpu.VMEM((3, NZ, BLK, FS), BF),
            pltpu.VMEM((2, NZ, BLK, FS), BF),
            pltpu.VMEM((2, PT, FS), BF),
            pltpu.VMEM((2, PT, FS), BF),
            pltpu.VMEM((2, PT, FS), BF),
            pltpu.VMEM((2, NP, TOK, FS), F32),
            pltpu.VMEM((2, NP, TOK, FS), F32),
            dma((1,)), dma((1,)), dma((1,)), dma((1,)), dma((2,)), dma((2,)),
            dma((2 + NX,)), dma((2 + NX,)), dma((2 + NX,)),
            dma((1,)), dma((1,)), dma((1,)), dma((2, NH, NX - 1)), dma((2, NH, NX - 1)),
            dma((2,)), dma((2, NH, NB)),
            dma((2, NH, NX - 1)), dma((2, NH, NX - 1)), dma((2, NH)), dma((2, NH)),
            dma((NH, NX - 1)), dma((NH, NX - 1, NB // GRP)), dma((2, NH)), dma((3,)),
            dma((2,)), dma((2,)), dma((2,)), dma((2,)), dma((2,)), dma((2,)),
        ],
        compiler_params=pltpu.CompilerParams(
            collective_id=0, has_side_effects=True, vmem_limit_bytes=56 * 2**20
        ),
    )(tokens_fwd, tokens_rev, *small, norm_gain, gate_proj, up_proj, down_proj)
    one = jax.ShapeDtypeStruct((1, TOK, D), BF)
    return pl.pallas_call(
        split, name="split", out_shape=(one, one), in_specs=[vmem], out_specs=(vmem, vmem)
    )(both)


def solution(mesh):
    placed = (
        P("expert", None),
        P("expert", None),
        P("section", "expert", None),
        P("section", "expert", None),
        P("section", "expert", None),
        P("section", "expert", None),
        P("section", None),
        P("section", None, "expert"),
        P("section", None, "expert"),
        P("section", "expert", None),
    )
    return jax.shard_map(
        run,
        mesh=mesh,
        in_specs=placed,
        out_specs=(P("section", "expert", None), P("section", "expert", None)),
        check_vma=False,
    )
```

time: 151 us -> 141 us (0.934)
  Pallas kernels: 148 us -> 141 us
  local copies, waits for them, and re-layouts: 3.1 us -> 0 us
    pallas_call x1 -> x2, Pallas kernels: 148 us -> 141 us  [the longest x1 139 us: run(): pl.pallas_call(kernel, name='moe_pipeline', out_shape=out, in_specs=[hbm]...]
    unnamed x2 -> x0, local copies, waits for them, and re-layouts: 3.1 us -> none
where the time goes in v3:
time: 141 us
  Pallas kernels  141 us (100%)
    pallas_call x1, Pallas kernels, run(): pl.pallas_call(kernel, name='moe_pipeline', out_shape=out, in_specs=[hbm]...  139 us

profile of v3, /device:TPU:33, one launch (start us, length us, event | category | flops | bytes accessed | tf_op | source)
XLA Modules:
  0.0 141.3 jit_solution(17278004098343135355)
XLA Ops:
  0.6 139.0 %moe_pipeline.1.both_ref = bf16[16,7168]{1,0:T(8,128)(2,1)} custom-call(bf16[8,7168]{1,0:T(8,128)(2,1)} %tokf_hbm.1, bf16[8,7168]{1,0:T(8,128)(2,1)} %tokr_hbm.1, s32[2,8]{1,0:T(2,128)} %bitcast.12, s32[2,8]{1,0:T(2,128)} %bitcast.13, bf16[2,8]{1,0:T(2,128)(2,1)} %bitcast.14, bf16[2,8]{1,0:T(2,128)(2,1)} %bitcast.15, bf16[1,7168]{1,0:T(2,128)(2,1)} %gain_hbm.1, ...), custom_call_target="tpu_custom_call" | custom-call | tf_op jit(solution)/shard_map/moe_pipeline/pallas_call | solution.py:558
  139.6 1.6 %split.1 = (bf16[1,8,7168]{2,1,0:T(8,128)(2,1)}, bf16[1,8,7168]{2,1,0:T(8,128)(2,1)}) custom-call(bf16[16,7168]{1,0:T(8,128)(2,1)} %moe_pipeline.1.both_ref), custom_call_target="tpu_custom_call" | custom-call | tf_op jit(solution)/shard_map/split/pallas_call | solution.py:614

commit v4 on v3

--- a/solution.py
+++ b/solution.py
@@ -21,17 +21,29 @@
 ROWS = NZ * NP * SLOT
 BLK = NP * SLOT
 PT = NP * TOK
+HALFWAY = 512
 NH = 2
 NB = NZ // NH
 HROWS = ROWS // NH
-OFFSETS = ((4, 2, 6, 0), (3, 5, 1, 7))
-FAR_FIRST = (4, 3, 5, 2, 6, 1, 7, 0)
-GRP = 1
+GROWS = HROWS // 2
+OFFSETS = ((0, 2, 6, 4), (1, 7, 3, 5))
+NEAR_FIRST = (1, 7, 2, 6, 3, 5, 4)
+FAR_BLOCKS = (3, 1, 2, 0)
 BF, F32 = jnp.bfloat16, jnp.float32
 
 
 def place(k):
     return OFFSETS[k % NH].index(-k % NZ)
+
+
+def pack(value):
+    return jnp.concatenate([value[:, 0:HALFWAY], value[:, FS - HALFWAY : FS]], axis=0).astype(BF)
+
+
+def unpack(packed, ref, start):
+    value = packed.astype(F32)
+    ref[:, start : start + HALFWAY] = value[0:TOK]
+    ref[:, start + FS - HALFWAY : start + FS] = value[TOK : 2 * TOK]
 
 
 def nt_dot(a, b):
@@ -42,7 +54,7 @@
     tokf_hbm, tokr_hbm, rf_hbm, rr_hbm, wf_hbm, wr_hbm, gain_hbm, gate_hbm, up_hbm, down_hbm,
     out_ref,
     tok_ref, rf_ref, rr_ref, wf_ref, wr_ref, gain_ref, out_f32, in_s,
-    wg, wu, wd, wall, tall, tokx, xin, sown, wcomb, wbefore, rin, acc, ssq, guout, guin, act, actin,
+    wg, wu, wd, wall, tall, tokx, xin, plane32, sown, wcomb, wbefore, rin, acc, ssq, guout, guin, act, actin,
     pout, pown, pin, ret, retin, dout, xcur, xres, xback, st_out, st_in,
     t_ss, t_rs, tok_ss, tok_rs, s_ss, s_rs, wl_s, w_ss, w_rs, wa_l, wa_ss, wa_rs, a_ss, a_rs,
     d_ss, d_rs, ag_ss, ag_rs, gu_ss, gu_rs, p_ss, p_rs, r_ss, r_rs, x_ss, x_rs, xb_ss, xb_rs, st_ss, st_rs,
@@ -80,6 +92,16 @@
             return carry
 
         lax.fori_loop(0, n, step, 0)
+
+    bar = pltpu.get_barrier_semaphore()
+
+    def greet(dev):
+        pl.semaphore_signal(bar, inc=1, device_id=dev, device_id_type=MESH)
+
+    loop(NP - 1, lambda r: greet(plane(r + 1)))
+    loop(NZ - 1, lambda k: greet(zpeer(k + 1)))
+    loop(NZ, lambda k: greet(at(up_sec, (z + k) % NZ, p)))
+    loop(NZ, lambda k: greet(at(down_sec, (z + k) % NZ, p)))
 
     small = [
         pltpu.make_async_copy(src, dst, in_s.at[n])
@@ -92,15 +114,6 @@
     tokens = [pltpu.make_async_copy(src, tok_ref, in_s.at[5]) for src in (tokf_hbm, tokr_hbm)]
     pl.when(s == 0)(lambda: tokens[0].start())
     pl.when(s == NS - 1)(lambda: tokens[1].start())
-    bar = pltpu.get_barrier_semaphore()
-
-    def greet(dev):
-        pl.semaphore_signal(bar, inc=1, device_id=dev, device_id_type=MESH)
-
-    loop(NP - 1, lambda r: greet(plane(r + 1)))
-    loop(NZ - 1, lambda k: greet(zpeer(k + 1)))
-    loop(NZ, lambda k: greet(at(up_sec, (z + k) % NZ, p)))
-    loop(NZ, lambda k: greet(at(down_sec, (z + k) % NZ, p)))
 
     def half(core):
         return pl.ds(core * HALF, HALF)
@@ -177,7 +190,7 @@
         for q in range(NP):
             f = (q % NC) * NX + q // NC
             sl = slice(f * FS, (f + 1) * FS)
-            tokx[q] = tok_ref[:, sl].astype(F32)
+            tokx[q] = pack(tok_ref[:, sl].astype(F32))
 
     pl.semaphore_wait(bar, NP - 1 + NZ - 1 + 2 * NZ)
 
@@ -243,7 +256,9 @@
     @pl.when(outer)
     def _():
         remote(tokx.at[few], xin.at[few], tok_ss.at[0], tok_rs.at[0], sib).wait_recv()
-        xcur[0] = xin[...].reshape(PT, FS).astype(BF)
+        for q in range(NP):
+            unpack(xin[q], plane32.at[q], 0)
+        xcur[0] = plane32[...].reshape(PT, FS).astype(BF)
 
     mine = z % NH
 
@@ -253,7 +268,9 @@
         )
 
     def stash(j, value):
-        st_out[j] = value.astype(F32).reshape(NP, TOK, FS)
+        value = value.astype(F32).reshape(NP, TOK, FS)
+        for q in range(NP):
+            st_out[j, q] = pack(value[q])
         st_in[j, p] = st_out[j, p]
         loop(NP - 1, lambda r: st_copy(j, r).start())
 
@@ -261,7 +278,7 @@
         remote(st_out.at[j, few], st_in.at[j, few], st_ss.at[j], st_rs.at[j], sib).wait_recv()
         for q in range(NP):
             f = (q % NC) * NX + q // NC
-            out_f32[j, :, f * FS : (f + 1) * FS] = st_in[j, q]
+            unpack(st_in[j, q], out_f32.at[j], f * FS)
 
     def stash_back(j):
         remote(xback.at[j], xback.at[j], xb_ss.at[j], xb_rs.at[j], zpeer(4)).wait_recv()
@@ -293,11 +310,11 @@
 
         picked = jnp.dot(sown[b, :, 0:PT], xcur[j], preferred_element_type=F32).astype(BF)
         dout[j] = picked.reshape(NZ, BLK, FS)
-        for k in FAR_FIRST[:-1]:
+        rin[j, mine, 0, place(0)] = picked[0:BLK]
+        for k in NEAR_FIRST:
             remote(
                 dout.at[j, k], rin.at[j, mine, 0, place(k)], d_ss.at[j], d_rs.at[j, mine, place(k)], zpeer(k)
             ).start()
-        rin[j, mine, 0, place(0)] = picked[0:BLK]
 
         @pl.when(has_next)
         def _():
@@ -359,17 +376,19 @@
             ssq[...] = ssq[...] + ss if d else ss
 
         def p_copy(h, d, g):
-            ks = pl.ds(g * GRP, GRP)
             return remote(
-                pout.at[h, d - 1, ks], pin.at[h, d - 1, ks], p_ss.at[h, d - 1], p_rs.at[h, d - 1, g], xpeer(d)
+                pout.at[h, d - 1, g], pin.at[h, d - 1, g], p_ss.at[h, d - 1], p_rs.at[h, d - 1, g], xpeer(d)
             )
 
-        def act_copy(h, d):
-            return remote(act.at[j, h], actin.at[j, h, d - 1], a_ss.at[j, h, d - 1], a_rs.at[j, h, d - 1], xpeer(d))
+        def act_copy(h, d, g):
+            rows = pl.ds(g * GROWS, GROWS)
+            return remote(
+                act.at[j, h, rows], actin.at[j, h, d - 1, rows], a_ss.at[j, h], a_rs.at[j, h, d - 1, g], xpeer(d)
+            )
 
         def all_of(value, q):
             w = wall[pl.ds(q * NC, NC)].reshape(NC * PIECE, FS)
-            return jnp.dot(value, w, preferred_element_type=F32).reshape(NB, BLK, FS)
+            return jnp.dot(value, w, preferred_element_type=F32).reshape(-1, BLK, FS)
 
         def expert(h):
             slice_product(h, 0)
@@ -401,15 +420,16 @@
                 for d in (2, 1, 3):
                     part = jnp.dot(act[j, h], wd[(x + d) % NX], preferred_element_type=F32)
                     pout[h, d - 1] = part.astype(BF).reshape(NB, BLK, FS)
-                for g in range(NB // GRP):
+                for g in FAR_BLOCKS:
                     for d in (2, 1, 3):
                         p_copy(h, d, g).start()
                 pown[h] = jnp.dot(act[j, h], wd[x], preferred_element_type=F32).reshape(NB, BLK, FS)
 
             @pl.when(jnp.logical_not(initial))
             def _():
-                for d in (2, 1, 3):
-                    act_copy(h, d).start()
+                for g in (1, 0):
+                    for d in (2, 1, 3):
+                        act_copy(h, d, g).start()
                 if h == 0:
                     pl.when((j == 0) | outer)(wait_spread)
                 pown[h] = all_of(act[j, h], x)
@@ -446,23 +466,25 @@
         def give_back(h):
             @pl.when(initial)
             def _():
-                for g in range(NB // GRP):
+                for m in FAR_BLOCKS:
                     for d in (1, 3, 2):
-                        p_copy(h, d, g).wait_recv()
-                    for m in range(g * GRP, (g + 1) * GRP):
-                        total = pown[h, m]
-                        for d in (1, 2, 3):
-                            total = total + pin[h, d - 1, m].astype(F32)
-                        hand(h, m, total)
+                        p_copy(h, d, m).wait_recv()
+                    total = pown[h, m]
+                    for d in (1, 2, 3):
+                        total = total + pin[h, d - 1, m].astype(F32)
+                    hand(h, m, total)
 
             @pl.when(jnp.logical_not(initial))
             def _():
-                total = pown[h]
-                for d in (1, 3, 2):
-                    act_copy(h, d).wait_recv()
-                    total = total + all_of(actin[j, h, d - 1], (x + NX - d) % NX)
-                for m in range(NB):
-                    hand(h, m, total[m])
+                for g in (1, 0):
+                    ms = range(g * NB // 2, (g + 1) * NB // 2)
+                    total = pown[h, ms.start : ms.stop]
+                    for d in (1, 3, 2):
+                        act_copy(h, d, g).wait_recv()
+                        rows = slice(g * GROWS, (g + 1) * GROWS)
+                        total = total + all_of(actin[j, h, d - 1, rows], (x + NX - d) % NX)
+                    for m in ms[::-1]:
+                        hand(h, m, total[m - ms.start])
 
         for h in range(NH):
             give_back(h)
@@ -534,9 +556,8 @@
 
             @pl.when(jnp.logical_not(outer & (j == 0)))
             def _():
-                for d in (1, 2, 3):
-                    here = act.at[j, h]
-                    remote(here, here, a_ss.at[j, h, d - 1], a_rs.at[j, h, d - 1], xpeer(d)).wait_send()
+                here = actin.at[j, h]
+                remote(here, here, a_ss.at[j, h], a_rs.at[j, h, 0, 0], sib).wait_send()
 
             remote(guout.at[j, h], guin.at[j, h], gu_ss.at[j, h], gu_rs.at[j, h], sib).wait_send()
 
@@ -575,7 +596,8 @@
             pltpu.VMEM((NX, NC * PIECE, FS), BF),
             pltpu.VMEM((NP, PIECE, FS), BF),
             pltpu.VMEM((NP, 2 * TOK, 128), F32),
-            pltpu.VMEM((NP, TOK, FS), F32),
+            pltpu.VMEM((NP, 2 * TOK, HALFWAY), BF),
+            pltpu.VMEM((NP, 2 * TOK, HALFWAY), BF),
             pltpu.VMEM((NP, TOK, FS), F32),
             pltpu.VMEM((2, ROWS, 128), BF),
             pltpu.VMEM((2, PT, ROWS), BF),
@@ -596,14 +618,14 @@
             pltpu.VMEM((2, PT, FS), BF),
             pltpu.VMEM((2, PT, FS), BF),
             pltpu.VMEM((2, PT, FS), BF),
-            pltpu.VMEM((2, NP, TOK, FS), F32),
-            pltpu.VMEM((2, NP, TOK, FS), F32),
+            pltpu.VMEM((2, NP, 2 * TOK, HALFWAY), BF),
+            pltpu.VMEM((2, NP, 2 * TOK, HALFWAY), BF),
             dma((1,)), dma((1,)), dma((1,)), dma((1,)), dma((2,)), dma((2,)),
             dma((2 + NX,)), dma((2 + NX,)), dma((2 + NX,)),
-            dma((1,)), dma((1,)), dma((1,)), dma((2, NH, NX - 1)), dma((2, NH, NX - 1)),
+            dma((1,)), dma((1,)), dma((1,)), dma((2, NH)), dma((2, NH, NX - 1, 2)),
             dma((2,)), dma((2, NH, NB)),
             dma((2, NH, NX - 1)), dma((2, NH, NX - 1)), dma((2, NH)), dma((2, NH)),
-            dma((NH, NX - 1)), dma((NH, NX - 1, NB // GRP)), dma((2, NH)), dma((3,)),
+            dma((NH, NX - 1)), dma((NH, NX - 1, NB)), dma((2, NH)), dma((3,)),
             dma((2,)), dma((2,)), dma((2,)), dma((2,)), dma((2,)), dma((2,)),
         ],
         compiler_params=pltpu.CompilerParams(

time: 141 us -> 137 us (0.972)
  Pallas kernels: 141 us -> 136 us
    pallas_call x1, Pallas kernels: 139 us -> 134 us  [run(): pl.pallas_call(kernel, name='moe_pipeline', out_shape=out, in_specs=[hbm]...]
where the time goes in v4:
time: 137 us; the launch traced here: 136 us
  Pallas kernels  136 us (99%)
    pallas_call x1, Pallas kernels, run(): pl.pallas_call(kernel, name='moe_pipeline', out_shape=out, in_specs=[hbm]...  134 us

profile of v4, /device:TPU:33, one launch (start us, length us, event | category | flops | bytes accessed | tf_op | source)
XLA Modules:
  0.0 136.5 jit_solution(10798567015755638786)
XLA Ops:
  0.6 134.2 %moe_pipeline.1.both_ref = bf16[16,7168]{1,0:T(8,128)(2,1)} custom-call(bf16[8,7168]{1,0:T(8,128)(2,1)} %tokf_hbm.1, bf16[8,7168]{1,0:T(8,128)(2,1)} %tokr_hbm.1, s32[2,8]{1,0:T(2,128)} %bitcast.12, s32[2,8]{1,0:T(2,128)} %bitcast.13, bf16[2,8]{1,0:T(2,128)(2,1)} %bitcast.14, bf16[2,8]{1,0:T(2,128)(2,1)} %bitcast.15, bf16[1,7168]{1,0:T(2,128)(2,1)} %gain_hbm.1, ...), custom_call_target="tpu_custom_call" | custom-call | tf_op jit(solution)/shard_map/moe_pipeline/pallas_call | solution.py:579
  134.9 1.6 %split.1 = (bf16[1,8,7168]{2,1,0:T(8,128)(2,1)}, bf16[1,8,7168]{2,1,0:T(8,128)(2,1)}) custom-call(bf16[16,7168]{1,0:T(8,128)(2,1)} %moe_pipeline.1.both_ref), custom_call_target="tpu_custom_call" | custom-call | tf_op jit(solution)/shard_map/split/pallas_call | solution.py:636

commit v5 on v4

--- a/solution.py
+++ b/solution.py
@@ -25,7 +25,7 @@
 NH = 2
 NB = NZ // NH
 HROWS = ROWS // NH
-GROWS = HROWS // 2
+GROUPS = (2, 4)
 OFFSETS = ((0, 2, 6, 4), (1, 7, 3, 5))
 NEAR_FIRST = (1, 7, 2, 6, 3, 5, 4)
 FAR_BLOCKS = (3, 1, 2, 0)
@@ -64,6 +64,7 @@
     z, p = i // NP, i % NP
     x, c = p // NC, p % NC
     outer = (s == 0) | (s == NS - 1)
+    inner = jnp.logical_not(outer)
     low = s < NS // 2
 
     def at(sec, zz, pp):
@@ -79,6 +80,7 @@
         return at(s, (z + k) % NZ, p)
 
     sib = at(s, z, x * NC + 1 - c)
+    q_far = (x + 2) % NX
     up_sec, down_sec = (s + 1) % NS, (s + NS - 1) % NS
 
     def remote(src, dst, ss, rs, dev):
@@ -146,21 +148,31 @@
     def local_spread():
         return pltpu.make_async_copy(down_hbm.at[0, :, slice_of(x, c)], wall.at[p], wa_l.at[0])
 
-    def spread(r):
-        q = (p + r + 1) % NP
-        return remote(down_hbm.at[0, :, slice_of(q // NC, q % NC)], wall.at[p], wa_ss.at[0], wa_rs.at[0], plane(r + 1))
-
-    def all_spread():
-        some = wall.at[pl.ds(0, NP - 1)]
+    def spread(q):
+        return remote(
+            down_hbm.at[0, :, slice_of(q // NC, q % NC)], wall.at[p], wa_ss.at[0], wa_rs.at[0], at(s, z, q)
+        )
+
+    def all_spread(count):
+        some = wall.at[pl.ds(0, count)]
         return remote(some, some, wa_ss.at[0], wa_rs.at[0], sib)
 
     def start_spread():
         local_spread().start()
-        loop(NP - 1, lambda r: spread(r).start())
+        for d in (1, 3):
+            for o in range(NC):
+                spread((x + d) % NX * NC + o).start()
+        spread(x * NC + 1 - c).start()
+
+        @pl.when(outer)
+        def _():
+            for o in range(NC):
+                spread((x + 2) % NX * NC + o).start()
 
     def wait_spread():
         local_spread().wait()
-        all_spread().wait_recv()
+        pl.when(outer)(lambda: all_spread(NP - 1).wait_recv())
+        pl.when(inner)(lambda: all_spread(NP - 1 - NC).wait_recv())
 
     for cp in local_gate_up():
         cp.start()
@@ -169,6 +181,8 @@
     def _():
         for q in range(NX):
             local_down(q).start()
+
+    pl.when(inner)(lambda: local_down(q_far).start())
 
     for cp in small:
         cp.wait()
@@ -216,7 +230,11 @@
         for q in range(NX):
             sibling_down(q).start()
 
-    pl.when(jnp.logical_not(outer))(start_spread)
+    @pl.when(inner)
+    def _():
+        sibling_down(q_far).start()
+        start_spread()
+
 
     @pl.when(outer)
     def _():
@@ -351,6 +369,8 @@
         for h in range(NH):
             relay(h)
 
+        pl.when(j == 1)(lambda: stash_back(0))
+
         @pl.when(j == 0)
         def _():
             for cp in local_gate_up():
@@ -360,9 +380,10 @@
 
         wide, hid = 2 * NC * PIECE, NC * PIECE
 
-        def slice_product(h, d):
+        def slice_product(hs, d):
             q = (x + NX - d) % NX
-            rows = rin[j, h, d].reshape(HROWS, FS).astype(F32)
+            rows = rin[j, hs.start : hs.stop, d].reshape(-1, FS).astype(F32)
+            mine_rows = slice(hs.start * HROWS, hs.stop * HROWS)
             g = gain_ref[:, pl.ds(pl.multiple_of(c * HALF + q * FS, 128), FS)].astype(F32)
             ss = jnp.sum(rows * rows, axis=1, keepdims=True)
             u = (rows * g).astype(BF)
@@ -371,17 +392,18 @@
                 for o in range(NC):
                     sl = slice((n * NC + o) * PIECE, (n * NC + o + 1) * PIECE)
                     part = jnp.dot(u, w[o, at_row, :], preferred_element_type=F32)
-                    acc[:, sl] = acc[:, sl] + part if d else part
-            ss = jnp.broadcast_to(ss, (HROWS, 128))
-            ssq[...] = ssq[...] + ss if d else ss
+                    acc[mine_rows, sl] = acc[mine_rows, sl] + part if d else part
+            ss = jnp.broadcast_to(ss, (rows.shape[0], 128))
+            ssq[mine_rows] = ssq[mine_rows] + ss if d else ss
 
         def p_copy(h, d, g):
+            n = d - 1 - j
             return remote(
-                pout.at[h, d - 1, g], pin.at[h, d - 1, g], p_ss.at[h, d - 1], p_rs.at[h, d - 1, g], xpeer(d)
+                pout.at[h, n, g], pin.at[h, n, g], p_ss.at[h, n], p_rs.at[h, n, g], xpeer(d)
             )
 
         def act_copy(h, d, g):
-            rows = pl.ds(g * GROWS, GROWS)
+            rows = pl.ds(g * HROWS // GROUPS[h], HROWS // GROUPS[h])
             return remote(
                 act.at[j, h, rows], actin.at[j, h, d - 1, rows], a_ss.at[j, h], a_rs.at[j, h, d - 1, g], xpeer(d)
             )
@@ -390,25 +412,30 @@
             w = wall[pl.ds(q * NC, NC)].reshape(NC * PIECE, FS)
             return jnp.dot(value, w, preferred_element_type=F32).reshape(-1, BLK, FS)
 
-        def expert(h):
-            slice_product(h, 0)
+        def gu_copy(h):
+            return remote(guout.at[j, h], guin.at[j, h], gu_ss.at[j, h], gu_rs.at[j, h], sib)
+
+        def products(h):
             for d in (1, 3, 2):
                 remote(rin.at[j, h, 0], rin.at[j, h, d], ag_ss.at[j, h, d - 1], ag_rs.at[j, h, d - 1], sib).wait_recv()
-                slice_product(h, d)
-
-            guout[j, h, :, 0:wide] = acc[...].astype(BF)
-            ss = ssq[...]
+                slice_product(range(h, h + 1), d)
+            mine_rows = slice(h * HROWS, (h + 1) * HROWS)
+            guout[j, h, :, 0:wide] = acc[mine_rows].astype(BF)
+            ss = ssq[mine_rows]
             hi = ss.astype(BF)
             lo = (ss - hi.astype(F32)).astype(BF)
             lanes = lax.broadcasted_iota(jnp.int32, (HROWS, 128), 1)
             guout[j, h, :, wide:] = jnp.where(lanes == 0, hi, lo)
-            gu = remote(guout.at[j, h], guin.at[j, h], gu_ss.at[j, h], gu_rs.at[j, h], sib)
-            gu.start()
-            gu.wait_recv()
-            ss = ss[:, 0:1] + guin[j, h, :, wide : wide + 1].astype(F32) + guin[j, h, :, wide + 1 : wide + 2].astype(F32)
+            gu_copy(h).start()
+
+        def activation(h):
+            gu_copy(h).wait_recv()
+            mine_rows = slice(h * HROWS, (h + 1) * HROWS)
+            ss = ssq[mine_rows, 0:1]
+            ss = ss + guin[j, h, :, wide : wide + 1].astype(F32) + guin[j, h, :, wide + 1 : wide + 2].astype(F32)
             scale = lax.rsqrt(ss * (1.0 / D) + 1e-06)
-            gate = (acc[:, 0:hid] + guin[j, h, :, 0:hid].astype(F32)) * scale
-            upv = (acc[:, hid:wide] + guin[j, h, :, hid:wide].astype(F32)) * scale
+            gate = (acc[mine_rows, 0:hid] + guin[j, h, :, 0:hid].astype(F32)) * scale
+            upv = (acc[mine_rows, hid:wide] + guin[j, h, :, hid:wide].astype(F32)) * scale
             act[j, h] = (gate / (1.0 + jnp.exp(-gate)) * upv).astype(BF)
 
             @pl.when(initial)
@@ -425,19 +452,40 @@
                         p_copy(h, d, g).start()
                 pown[h] = jnp.dot(act[j, h], wd[x], preferred_element_type=F32).reshape(NB, BLK, FS)
 
+            @pl.when(inner)
+            def _():
+                if h == 0:
+
+                    @pl.when(j == 0)
+                    def _():
+                        local_down(q_far).wait()
+                        sibling_down(q_far).wait_recv()
+
+                part = jnp.dot(act[j, h], wd[q_far], preferred_element_type=F32)
+                pout[h, 1 - j] = part.astype(BF).reshape(NB, BLK, FS)
+                for g in FAR_BLOCKS:
+                    p_copy(h, 2, g).start()
+
             @pl.when(jnp.logical_not(initial))
             def _():
-                for g in (1, 0):
-                    for d in (2, 1, 3):
+                for g in range(GROUPS[h] - 1, -1, -1):
+                    pl.when(outer)(lambda: act_copy(h, 2, g).start())
+                    for d in (1, 3):
                         act_copy(h, d, g).start()
+
+        def own_product(h):
+            @pl.when(jnp.logical_not(initial))
+            def _():
                 if h == 0:
                     pl.when((j == 0) | outer)(wait_spread)
                 pown[h] = all_of(act[j, h], x)
 
-        for h in range(NH):
-            expert(h)
-
-        pl.when(j == 1)(lambda: stash_back(0))
+        slice_product(range(NH), 0)
+        products(0)
+        activation(0)
+        products(1)
+        own_product(0)
+        activation(1)
 
         def r_copy(h, m, k):
             kk = (NZ - k) % NZ
@@ -476,18 +524,32 @@
 
             @pl.when(jnp.logical_not(initial))
             def _():
-                for g in (1, 0):
-                    ms = range(g * NB // 2, (g + 1) * NB // 2)
+                for g in range(GROUPS[h] - 1, -1, -1):
+                    ms = range(g * NB // GROUPS[h], (g + 1) * NB // GROUPS[h])
                     total = pown[h, ms.start : ms.stop]
-                    for d in (1, 3, 2):
+                    rows = slice(ms.start * BLK, ms.stop * BLK)
+
+                    def add_chip(total, d):
                         act_copy(h, d, g).wait_recv()
-                        rows = slice(g * GROWS, (g + 1) * GROWS)
-                        total = total + all_of(actin[j, h, d - 1, rows], (x + NX - d) % NX)
-                    for m in ms[::-1]:
-                        hand(h, m, total[m - ms.start])
-
-        for h in range(NH):
-            give_back(h)
+                        return total + all_of(actin[j, h, d - 1, rows], (x + NX - d) % NX)
+
+                    total = add_chip(add_chip(total, 1), 3)
+
+                    @pl.when(outer)
+                    def _():
+                        whole = add_chip(total, 2)
+                        for m in ms[::-1]:
+                            hand(h, m, whole[m - ms.start])
+
+                    @pl.when(inner)
+                    def _():
+                        for m in ms[::-1]:
+                            p_copy(h, 2, m).wait_recv()
+                            hand(h, m, total[m - ms.start] + pin[h, 1 - j, m].astype(F32))
+
+        give_back(0)
+        own_product(1)
+        give_back(1)
         pl.when(initial)(w_wait)
         pl.when(initial)(start_spread)
         pl.when(j == 1)(lambda: finish(0))
@@ -516,7 +578,9 @@
         w_copy(b).wait_send()
     for cp in sibling_gate_up():
         cp.wait_send()
-    all_spread().wait_send()
+    pl.when(inner)(lambda: sibling_down(q_far).wait_send())
+    pl.when(outer)(lambda: all_spread(NP - 1).wait_send())
+    pl.when(inner)(lambda: all_spread(NP - 1 - NC).wait_send())
 
     @pl.when(outer)
     def _():
@@ -556,8 +620,17 @@
 
             @pl.when(jnp.logical_not(outer & (j == 0)))
             def _():
-                here = actin.at[j, h]
-                remote(here, here, a_ss.at[j, h], a_rs.at[j, h, 0, 0], sib).wait_send()
+                def act_sent(count):
+                    here = actin.at[j, h, pl.ds(0, count)]
+                    remote(here, here, a_ss.at[j, h], a_rs.at[j, h, 0, 0], sib).wait_send()
+
+                pl.when(outer)(lambda: act_sent(NX - 1))
+
+                @pl.when(inner)
+                def _():
+                    act_sent(2)
+                    here = pout.at[h, 1 - j]
+                    remote(here, here, p_ss.at[h, 1 - j], p_rs.at[h, 1 - j, 0], xpeer(2)).wait_send()
 
             remote(guout.at[j, h], guin.at[j, h], gu_ss.at[j, h], gu_rs.at[j, h], sib).wait_send()
 
@@ -603,8 +676,8 @@
             pltpu.VMEM((2, PT, ROWS), BF),
             pltpu.VMEM((2, PT, ROWS), BF),
             pltpu.VMEM((2, NH, NX, NB, BLK, FS), BF),
-            pltpu.VMEM((HROWS, wide), F32),
-            pltpu.VMEM((HROWS, 128), F32),
+            pltpu.VMEM((ROWS, wide), F32),
+            pltpu.VMEM((ROWS, 128), F32),
             pltpu.VMEM((2, NH, HROWS, wide + 128), BF),
             pltpu.VMEM((2, NH, HROWS, wide + 128), BF),
             pltpu.VMEM((2, NH, HROWS, NC * PIECE), BF),
@@ -622,7 +695,7 @@
             pltpu.VMEM((2, NP, 2 * TOK, HALFWAY), BF),
             dma((1,)), dma((1,)), dma((1,)), dma((1,)), dma((2,)), dma((2,)),
             dma((2 + NX,)), dma((2 + NX,)), dma((2 + NX,)),
-            dma((1,)), dma((1,)), dma((1,)), dma((2, NH)), dma((2, NH, NX - 1, 2)),
+            dma((1,)), dma((1,)), dma((1,)), dma((2, NH)), dma((2, NH, NX - 1, max(GROUPS))),
             dma((2,)), dma((2, NH, NB)),
             dma((2, NH, NX - 1)), dma((2, NH, NX - 1)), dma((2, NH)), dma((2, NH)),
             dma((NH, NX - 1)), dma((NH, NX - 1, NB)), dma((2, NH)), dma((3,)),
@@ -632,10 +705,7 @@
             collective_id=0, has_side_effects=True, vmem_limit_bytes=56 * 2**20
         ),
     )(tokens_fwd, tokens_rev, *small, norm_gain, gate_proj, up_proj, down_proj)
-    one = jax.ShapeDtypeStruct((1, TOK, D), BF)
-    return pl.pallas_call(
-        split, name="split", out_shape=(one, one), in_specs=[vmem], out_specs=(vmem, vmem)
-    )(both)
+    return both[None, 0:TOK], both[None, TOK : 2 * TOK]
 
 
 def solution(mesh):

time: 137 us -> 136 us (level)
  Pallas kernels: 136 us -> 134 us
  local copies, waits for them, and re-layouts: 0 us -> 1.65 us
    broadcast_in_dim x0 -> x1, local copies, waits for them, and re-layouts: none -> 1.65 us  [run(): return (both[None, 0:TOK], both[None, TOK:2 * TOK])]
    pallas_call x1 -> x0, Pallas kernels: 1.63 us -> none  [run(): pl.pallas_call(split, name='split', out_shape=(one, one), in_specs=[vmem]...]
where the time goes in v5:
time: 136 us
  Pallas kernels  134 us (99%)
  local copies, waits for them, and re-layouts  1.65 us (1%)
    pallas_call x1, Pallas kernels, run(): pl.pallas_call(kernel, name='moe_pipeline', out_shape=out, in_specs=[hbm]...  134 us

profile of v5, /device:TPU:33, one launch (start us, length us, event | category | flops | bytes accessed | tf_op | source)
XLA Modules:
  0.0 135.8 jit_solution(13577858184323709449)
XLA Ops:
  0.6 133.5 %moe_pipeline.1 = bf16[16,7168]{1,0:T(8,128)(2,1)} custom-call(bf16[8,7168]{1,0:T(8,128)(2,1)} %tokf_hbm.1, bf16[8,7168]{1,0:T(8,128)(2,1)} %tokr_hbm.1, s32[2,8]{1,0:T(2,128)} %bitcast.16, s32[2,8]{1,0:T(2,128)} %bitcast.17, bf16[2,8]{1,0:T(2,128)(2,1)} %bitcast.18, bf16[2,8]{1,0:T(2,128)(2,1)} %bitcast.19, bf16[1,7168]{1,0:T(2,128)(2,1)} %gain_hbm.1, ...), custom_call_target="tpu_custom_call" | custom-call | tf_op jit(solution)/shard_map/moe_pipeline/pallas_call | solution.py:652
  134.2 1.7 %slice_bitcast_fusion = (bf16[1,8,7168]{2,1,0:T(8,128)(2,1)}, bf16[1,8,7168]{2,1,0:T(8,128)(2,1)}) fusion(bf16[16,7168]{1,0:T(8,128)(2,1)} %moe_pipeline.1), kind=kLoop, calls=%fused_computation | loop fusion | bytes 458752 | tf_op jit(solution)/shard_map/broadcast_in_dim | solution.py:708

commit v6 on v5

--- a/solution.py
+++ b/solution.py
@@ -51,9 +51,9 @@
 
 
 def kernel(
-    tokf_hbm, tokr_hbm, rf_hbm, rr_hbm, wf_hbm, wr_hbm, gain_hbm, gate_hbm, up_hbm, down_hbm,
+    tokf_ref, tokr_ref, rf_ref, rr_ref, wf_ref, wr_ref, gain_ref, gate_hbm, up_hbm, down_hbm,
     out_ref,
-    tok_ref, rf_ref, rr_ref, wf_ref, wr_ref, gain_ref, out_f32, in_s,
+    out_f32,
     wg, wu, wd, wall, tall, tokx, xin, plane32, sown, wcomb, wbefore, rin, acc, ssq, guout, guin, act, actin,
     pout, pown, pin, ret, retin, dout, xcur, xres, xback, st_out, st_in,
     t_ss, t_rs, tok_ss, tok_rs, s_ss, s_rs, wl_s, w_ss, w_rs, wa_l, wa_ss, wa_rs, a_ss, a_rs,
@@ -105,18 +105,6 @@
     loop(NZ, lambda k: greet(at(up_sec, (z + k) % NZ, p)))
     loop(NZ, lambda k: greet(at(down_sec, (z + k) % NZ, p)))
 
-    small = [
-        pltpu.make_async_copy(src, dst, in_s.at[n])
-        for n, (src, dst) in enumerate(
-            ((rf_hbm, rf_ref), (rr_hbm, rr_ref), (wf_hbm, wf_ref), (wr_hbm, wr_ref), (gain_hbm, gain_ref))
-        )
-    ]
-    for cp in small:
-        cp.start()
-    tokens = [pltpu.make_async_copy(src, tok_ref, in_s.at[5]) for src in (tokf_hbm, tokr_hbm)]
-    pl.when(s == 0)(lambda: tokens[0].start())
-    pl.when(s == NS - 1)(lambda: tokens[1].start())
-
     def half(core):
         return pl.ds(core * HALF, HALF)
 
@@ -184,8 +172,6 @@
 
     pl.when(inner)(lambda: local_down(q_far).start())
 
-    for cp in small:
-        cp.wait()
     ei = lax.broadcasted_iota(jnp.int32, (2 * LIVE, TOK), 0)
     eye = jnp.where(
         lax.broadcasted_iota(jnp.int32, (TOK, TOK), 0) == lax.broadcasted_iota(jnp.int32, (TOK, TOK), 1), 1.0, 0.0
@@ -200,11 +186,10 @@
 
     @pl.when(outer)
     def _():
-        tokens[0].wait()
         for q in range(NP):
             f = (q % NC) * NX + q // NC
             sl = slice(f * FS, (f + 1) * FS)
-            tokx[q] = pack(tok_ref[:, sl].astype(F32))
+            tokx[q] = pack(jnp.where(s == 0, tokf_ref[:, sl].astype(F32), tokr_ref[:, sl].astype(F32)))
 
     pl.semaphore_wait(bar, NP - 1 + NZ - 1 + 2 * NZ)
 
@@ -568,8 +553,7 @@
 
     finish(1)
     jf = jnp.where(low, 0, 1)
-    out_ref[0:TOK, :] = out_f32[jf].astype(BF)
-    out_ref[TOK : 2 * TOK, :] = out_f32[1 - jf].astype(BF)
+    out_ref[...] = jnp.concatenate([out_f32[jf], out_f32[1 - jf]], axis=0).astype(BF)
 
     for j in range(2):
         remote(st_out.at[j, few], st_in.at[j, few], st_ss.at[j], st_rs.at[j], sib).wait_send()
@@ -653,17 +637,10 @@
         kernel,
         name="moe_pipeline",
         out_shape=out,
-        in_specs=[hbm] * 10,
+        in_specs=[vmem] * 7 + [hbm] * 3,
         out_specs=vmem,
         scratch_shapes=[
-            pltpu.VMEM((TOK, D), BF),
-            pltpu.VMEM((TOPK, TOK), jnp.int32),
-            pltpu.VMEM((TOPK, TOK), jnp.int32),
-            pltpu.VMEM((TOPK, TOK), BF),
-            pltpu.VMEM((TOPK, TOK), BF),
-            pltpu.VMEM((1, D), BF),
             pltpu.VMEM((2, TOK, D), F32),
-            dma((6,)),
             pltpu.VMEM((NC, HALF, PIECE), BF),
             pltpu.VMEM((NC, HALF, PIECE), BF),
             pltpu.VMEM((NX, NC * PIECE, FS), BF),

time: 136 us -> 136 us (level)
  no operation moved by 1% of the time
where the time goes in v6:
time: 136 us
  Pallas kernels  134 us (99%)
  local copies, waits for them, and re-layouts  1.65 us (1%)
    pallas_call x1, Pallas kernels, run(): pl.pallas_call(kernel, name='moe_pipeline', out_shape=out, in_specs=[vmem...  134 us

profile of v6, /device:TPU:33, one launch (start us, length us, event | category | flops | bytes accessed | tf_op | source)
XLA Modules:
  0.0 135.9 jit_solution(2346560122541994652)
XLA Ops:
  0.6 133.6 %moe_pipeline.1 = bf16[16,7168]{1,0:T(8,128)(2,1)} custom-call(bf16[8,7168]{1,0:T(8,128)(2,1)} %tokf_ref.1, bf16[8,7168]{1,0:T(8,128)(2,1)} %tokr_ref.1, s32[2,8]{1,0:T(2,128)} %bitcast.16, s32[2,8]{1,0:T(2,128)} %bitcast.17, bf16[2,8]{1,0:T(2,128)(2,1)} %bitcast.18, bf16[2,8]{1,0:T(2,128)(2,1)} %bitcast.19, bf16[1,7168]{1,0:T(2,128)(2,1)} %gain_ref.1, ...), custom_call_target="tpu_custom_call" | custom-call | tf_op jit(solution)/shard_map/moe_pipeline/pallas_call | solution.py:636
  134.2 1.7 %slice_bitcast_fusion = (bf16[1,8,7168]{2,1,0:T(8,128)(2,1)}, bf16[1,8,7168]{2,1,0:T(8,128)(2,1)}) fusion(bf16[16,7168]{1,0:T(8,128)(2,1)} %moe_pipeline.1), kind=kLoop, calls=%fused_computation | loop fusion | bytes 458752 | tf_op jit(solution)/shard_map/broadcast_in_dim | solution.py:685
